TPU v7x, 128 devices: a whole 4x4x4 slice. The times are simulated.
128 devices in a mesh: replica: 8 (over x, core), fsdp: 16 (over y, z).
Axes of the slice: x: 4, y: 4, z: 4, core: 2. Of those that a mesh axis runs over, the one named last changes fastest.
Arguments:
- tokens: bfloat16 [16384, 1024], P(('replica', 'fsdp')), may hold values from -6 to 6
- lengths: int32 [8, 4], P('replica'), may hold values from 1 to 2045, as said below
- cotangent: bfloat16 [16384, 1024], P(('replica', 'fsdp')), may hold values from -6 to 6
- attention_gain: bfloat16 [1024], P('fsdp'), may hold values from 0.099609375 to 1.8984375
- query_weight: bfloat16 [1024, 1024], P('fsdp'), may hold values from -0.1875 to 0.1875
- key_weight: bfloat16 [1024, 512], P('fsdp'), may hold values from -0.1875 to 0.1875
- value_weight: bfloat16 [1024, 512], P('fsdp'), may hold values from -0.1875 to 0.1875
- query_gain: bfloat16 [64], P('fsdp'), may hold values from 0.099609375 to 1.8984375
- key_gain: bfloat16 [64], P('fsdp'), may hold values from 0.099609375 to 1.8984375
- out_weight: bfloat16 [1024, 1024], P('fsdp'), may hold values from -1.5 to 1.5
- middle_gain: bfloat16 [1024], P('fsdp'), may hold values from 0.099609375 to 1.8984375
- gate_weight: bfloat16 [1024, 4608], P(None, 'fsdp'), may hold values from -0.1875 to 0.1875
- up_weight: bfloat16 [1024, 4608], P(None, 'fsdp'), may hold values from -0.1875 to 0.1875
- down_weight: bfloat16 [4608, 1024], P('fsdp'), may hold values from -0.09375 to 0.09375
Outputs:
- block_output: bfloat16 [16384, 1024], P(('replica', 'fsdp'))
- tokens_grad: float32 [16384, 1024], P(('replica', 'fsdp'))
- attention_gain_grad: float32 [1024], P('fsdp')
- query_weight_grad: float32 [1024, 1024], P('fsdp')
- key_weight_grad: float32 [1024, 512], P('fsdp')
- value_weight_grad: float32 [1024, 512], P('fsdp')
- query_gain_grad: float32 [64], P('fsdp')
- key_gain_grad: float32 [64], P('fsdp')
- out_weight_grad: float32 [1024, 1024], P('fsdp')
- middle_gain_grad: float32 [1024], P('fsdp')
- gate_weight_grad: float32 [1024, 4608], P(None, 'fsdp')
- up_weight_grad: float32 [1024, 4608], P(None, 'fsdp')
- down_weight_grad: float32 [4608, 1024], P('fsdp')
Inputs may be any that keep to these rules, and one draw needn't show every extreme that they name: Each row's 4 lengths sum to 2048; all of them but one are at most 32.
All inputs are finite; a program needn't handle non-finite values.
Results may differ from a plain program's by a relative error of at most 0.025.
Values may be sent and summed in bfloat16 or wider, within the bound.
No kernel may reach another device: no remote copies, remote signals or barrier semaphores. Data moves between devices by JAX's collectives and lax.ppermute only.
A program may use at most 192 MiB of HBM per device.

v0:
```python
import math

import jax
import jax.numpy as jnp
from jax import lax
from jax.sharding import PartitionSpec as P

HEADS = 16
KV_HEADS = 8
HEAD_DIM = 64


epsilon = 1e-05
rope_base = 1000000.0
masked_score = -1e30


def normalize(source, gain):
    return source * lax.rsqrt(jnp.mean(source * source, axis=-1, keepdims=True) + epsilon) * gain


def rotate(source, cosine, sine):
    middle_at = source.shape[-1] // 2
    first_half = source[..., :middle_at]
    second_half = source[..., middle_at:]
    return jnp.concatenate(
        [first_half * cosine - second_half * sine, second_half * cosine + first_half * sine],
        axis=-1,
    )


def tables(position):
    steps_half = jnp.arange(HEAD_DIM // 2, dtype=jnp.float32)
    inverse = rope_base ** (-2.0 * steps_half / HEAD_DIM)
    angles = position.astype(jnp.float32)[:, None] * inverse[None, :]
    return (jnp.cos(angles)[:, None, :], jnp.sin(angles)[:, None, :])


def locate(places, seq_lengths):
    ends = jnp.cumsum(seq_lengths)
    passed = (places[:, None] >= ends[None, :]).astype(jnp.int32)
    document = jnp.sum(passed, axis=1)
    position = places - jnp.sum(passed * seq_lengths[None, :], axis=1)
    return (document, position)


def finish(raw_rows, gain, cosine, sine):
    shaped = raw_rows.reshape(raw_rows.shape[0], -1, HEAD_DIM)
    return rotate(normalize(shaped, gain), cosine, sine)


def gated(gate_part, up_part):
    return jax.nn.silu(gate_part) * up_part


def on_device(
    tokens,
    lengths,
    cotangent,
    attention_gain,
    query_weight,
    key_weight,
    value_weight,
    query_gain,
    key_gain,
    out_weight,
    middle_gain,
    gate_weight,
    up_weight,
    down_weight,
):
    row_count = tokens.shape[0]
    group_rows = row_count * lax.axis_size("fsdp")
    repeat = HEADS // KV_HEADS
    scale_factor = HEAD_DIM ** (-0.5)
    own_places = lax.axis_index("fsdp") * row_count + jnp.arange(row_count, dtype=jnp.int32)
    all_places = jnp.arange(group_rows, dtype=jnp.int32)
    own_doc, own_position = locate(own_places, lengths[0])
    key_doc = locate(all_places, lengths[0])[0]
    cosine, sine = tables(own_position)
    gain_in, gain_mid, gain_query, gain_key, w_query, w_key, w_value, w_out = (
        lax.all_gather(attention_gain, "fsdp", axis=0, tiled=True),
        lax.all_gather(middle_gain, "fsdp", axis=0, tiled=True),
        lax.all_gather(query_gain, "fsdp", axis=0, tiled=True),
        lax.all_gather(key_gain, "fsdp", axis=0, tiled=True),
        lax.all_gather(query_weight, "fsdp", axis=0, tiled=True),
        lax.all_gather(key_weight, "fsdp", axis=0, tiled=True),
        lax.all_gather(value_weight, "fsdp", axis=0, tiled=True),
        lax.all_gather(out_weight, "fsdp", axis=0, tiled=True),
    )
    gain_in = gain_in.astype(jnp.float32)
    gain_mid = gain_mid.astype(jnp.float32)
    gain_query = gain_query.astype(jnp.float32)
    gain_key = gain_key.astype(jnp.float32)
    inputs = tokens.astype(jnp.float32)
    normed_in = normalize(inputs, gain_in).astype(jnp.bfloat16)
    query_raw = jnp.dot(normed_in, w_query, preferred_element_type=jnp.float32)
    key_raw = jnp.dot(normed_in, w_key, preferred_element_type=jnp.float32)
    value_rows = (
        jnp.dot(normed_in, w_value, preferred_element_type=jnp.float32)
        .astype(jnp.bfloat16)
        .reshape(row_count, KV_HEADS, HEAD_DIM)
    )
    queries = (
        finish(query_raw, gain_query, cosine, sine)
        .astype(jnp.bfloat16)
        .reshape(row_count, KV_HEADS, repeat, HEAD_DIM)
    )
    own_keys = finish(key_raw, gain_key, cosine, sine).astype(jnp.bfloat16)
    all_keys, all_values = (
        lax.all_gather(own_keys, "fsdp", axis=0, tiled=True),
        lax.all_gather(value_rows, "fsdp", axis=0, tiled=True),
    )
    block_rows = math.gcd(512, group_rows)
    block_starts = jnp.arange(group_rows // block_rows, dtype=jnp.int32) * block_rows
    stat_shape = (row_count, KV_HEADS, repeat)

    def visible_at(block_start):
        block_doc = lax.dynamic_slice_in_dim(key_doc, block_start, block_rows, 0)
        block_places = block_start + jnp.arange(block_rows, dtype=jnp.int32)
        return (own_doc[:, None] == block_doc[None, :]) & (
            block_places[None, :] <= own_places[:, None]
        )

    def scores_at(block_start):
        key_block = lax.dynamic_slice_in_dim(all_keys, block_start, block_rows, 0)
        return (
            jnp.einsum("tgrd,jgd->tgrj", queries, key_block, preferred_element_type=jnp.float32)
            * scale_factor
        )

    def top_step(carry, block_start):
        visible = visible_at(block_start)

        def top_update(running):
            scores = jnp.where(visible[:, None, None, :], scores_at(block_start), masked_score)
            new_top = jnp.maximum(running[0], jnp.max(scores, axis=-1))
            new_total = running[1] * jnp.exp(running[0] - new_top) + jnp.sum(
                jnp.exp(scores - new_top[..., None]), axis=-1
            )
            return (new_top, new_total)

        return (lax.cond(jnp.any(visible), top_update, lambda unchanged: unchanged, carry), None)

    (row_top, row_total), ignored = lax.scan(
        top_step,
        (jnp.full(stat_shape, masked_score, jnp.float32), jnp.zeros(stat_shape, jnp.float32)),
        block_starts,
    )
    log_total = row_top + jnp.log(row_total)

    def probs_at(block_start, visible):
        return jnp.where(
            visible[:, None, None, :], jnp.exp(scores_at(block_start) - log_total[..., None]), 0.0
        )

    def out_step(carry, block_start):
        visible = visible_at(block_start)

        def out_update(accum):
            value_block = lax.dynamic_slice_in_dim(all_values, block_start, block_rows, 0)
            weights_low = probs_at(block_start, visible).astype(jnp.bfloat16)
            return accum + jnp.einsum(
                "tgrj,jgd->tgrd", weights_low, value_block, preferred_element_type=jnp.float32
            )

        return (lax.cond(jnp.any(visible), out_update, lambda unchanged: unchanged, carry), None)

    attended, ignored = lax.scan(
        out_step, jnp.zeros((row_count, KV_HEADS, repeat, HEAD_DIM), jnp.float32), block_starts
    )
    attended_low = attended.reshape(row_count, HEADS * HEAD_DIM).astype(jnp.bfloat16)
    middle = inputs + jnp.dot(attended_low, w_out, preferred_element_type=jnp.float32)
    normed_mid = normalize(middle, gain_mid).astype(jnp.bfloat16)
    w_gate, w_up, w_down = (
        lax.all_gather(gate_weight, "fsdp", axis=1, tiled=True),
        lax.all_gather(up_weight, "fsdp", axis=1, tiled=True),
        lax.all_gather(down_weight, "fsdp", axis=0, tiled=True),
    )
    gate_rows = jnp.dot(normed_mid, w_gate, preferred_element_type=jnp.float32)
    up_rows = jnp.dot(normed_mid, w_up, preferred_element_type=jnp.float32)
    hidden = gated(gate_rows, up_rows).astype(jnp.bfloat16)
    ffn_result = jnp.dot(hidden, w_down, preferred_element_type=jnp.float32)
    block_output = (middle + ffn_result).astype(jnp.bfloat16)
    d_hidden = jnp.dot(cotangent, w_down.T, preferred_element_type=jnp.float32)
    ignored, gated_back = jax.vjp(gated, gate_rows, up_rows)
    d_gate_raw, d_up_raw = gated_back(d_hidden)
    d_gate_low = d_gate_raw.astype(jnp.bfloat16)
    d_up_low = d_up_raw.astype(jnp.bfloat16)
    term_gate = jnp.dot(normed_mid.T, d_gate_low, preferred_element_type=jnp.float32)
    term_up = jnp.dot(normed_mid.T, d_up_low, preferred_element_type=jnp.float32)
    term_down = jnp.dot(hidden.T, cotangent, preferred_element_type=jnp.float32)
    grad_gate, grad_up, grad_down = (
        lax.psum_scatter(
            term_gate.astype(jnp.bfloat16), "fsdp", scatter_dimension=1, tiled=True
        ).astype(jnp.float32),
        lax.psum_scatter(
            term_up.astype(jnp.bfloat16), "fsdp", scatter_dimension=1, tiled=True
        ).astype(jnp.float32),
        lax.psum_scatter(
            term_down.astype(jnp.bfloat16), "fsdp", scatter_dimension=0, tiled=True
        ).astype(jnp.float32),
    )
    d_normed_mid = jnp.dot(d_gate_low, w_gate.T, preferred_element_type=jnp.float32) + jnp.dot(
        d_up_low, w_up.T, preferred_element_type=jnp.float32
    )
    ignored, norm_mid_back = jax.vjp(normalize, middle, gain_mid)
    d_middle_norm, d_gain_mid = norm_mid_back(d_normed_mid)
    d_middle = cotangent.astype(jnp.float32) + d_middle_norm
    d_middle_low = d_middle.astype(jnp.bfloat16)
    term_out = jnp.dot(attended_low.T, d_middle_low, preferred_element_type=jnp.float32)
    d_attended = (
        jnp.dot(d_middle_low, w_out.T, preferred_element_type=jnp.float32)
        .astype(jnp.bfloat16)
        .reshape(row_count, KV_HEADS, repeat, HEAD_DIM)
    )
    delta = jnp.sum(d_attended.astype(jnp.float32) * attended, axis=-1)

    def back_step(carry, block_start):
        visible = visible_at(block_start)

        def back_update(d_query):
            key_block = lax.dynamic_slice_in_dim(all_keys, block_start, block_rows, 0)
            value_block = lax.dynamic_slice_in_dim(all_values, block_start, block_rows, 0)
            probs = probs_at(block_start, visible)
            d_probs = jnp.einsum(
                "tgrd,jgd->tgrj", d_attended, value_block, preferred_element_type=jnp.float32
            )
            d_scores = (probs * (d_probs - delta[..., None])).astype(jnp.bfloat16)
            next_query = (
                d_query
                + jnp.einsum(
                    "tgrj,jgd->tgrd", d_scores, key_block, preferred_element_type=jnp.float32
                )
                * scale_factor
            )
            d_keys = (
                jnp.einsum("tgrj,tgrd->jgd", d_scores, queries, preferred_element_type=jnp.float32)
                * scale_factor
            )
            d_values = jnp.einsum(
                "tgrj,tgrd->jgd",
                probs.astype(jnp.bfloat16),
                d_attended,
                preferred_element_type=jnp.float32,
            )
            return (next_query, (d_keys, d_values))

        def skipped(d_query):
            empty_block = jnp.zeros((block_rows, KV_HEADS, HEAD_DIM), jnp.float32)
            return (d_query, (empty_block, empty_block))

        return lax.cond(jnp.any(visible), back_update, skipped, carry)

    d_queries, (key_terms, value_terms) = lax.scan(
        back_step, jnp.zeros((row_count, KV_HEADS, repeat, HEAD_DIM), jnp.float32), block_starts
    )
    key_terms = key_terms.reshape(group_rows, KV_HEADS, HEAD_DIM)
    value_terms = value_terms.reshape(group_rows, KV_HEADS, HEAD_DIM)
    key_grad, value_grad = (
        lax.psum_scatter(
            key_terms.astype(jnp.bfloat16), "fsdp", scatter_dimension=0, tiled=True
        ).astype(jnp.float32),
        lax.psum_scatter(
            value_terms.astype(jnp.bfloat16), "fsdp", scatter_dimension=0, tiled=True
        ).astype(jnp.float32),
    )
    ignored, query_back = jax.vjp(
        lambda raw_rows, head_gain: finish(raw_rows, head_gain, cosine, sine), query_raw, gain_query
    )
    d_query_raw, d_gain_query = query_back(d_queries.reshape(row_count, HEADS, HEAD_DIM))
    ignored, key_back = jax.vjp(
        lambda raw_rows, head_gain: finish(raw_rows, head_gain, cosine, sine), key_raw, gain_key
    )
    d_key_raw, d_gain_key = key_back(key_grad)
    d_query_low = d_query_raw.astype(jnp.bfloat16)
    d_key_low = d_key_raw.astype(jnp.bfloat16)
    d_value_low = value_grad.reshape(row_count, KV_HEADS * HEAD_DIM).astype(jnp.bfloat16)
    term_query = jnp.dot(normed_in.T, d_query_low, preferred_element_type=jnp.float32)
    term_key = jnp.dot(normed_in.T, d_key_low, preferred_element_type=jnp.float32)
    term_value = jnp.dot(normed_in.T, d_value_low, preferred_element_type=jnp.float32)
    d_normed_in = jnp.dot(d_query_low, w_query.T, preferred_element_type=jnp.float32)
    d_normed_in = d_normed_in + jnp.dot(d_key_low, w_key.T, preferred_element_type=jnp.float32)
    d_normed_in = d_normed_in + jnp.dot(d_value_low, w_value.T, preferred_element_type=jnp.float32)
    ignored, norm_in_back = jax.vjp(normalize, inputs, gain_in)
    d_inputs_norm, d_gain_in = norm_in_back(d_normed_in)
    tokens_grad = d_middle + d_inputs_norm
    (
        grad_in,
        grad_mid,
        grad_query_gain,
        grad_key_gain,
        grad_query,
        grad_key,
        grad_value,
        grad_out,
    ) = (
        lax.psum_scatter(
            d_gain_in.astype(jnp.bfloat16), "fsdp", scatter_dimension=0, tiled=True
        ).astype(jnp.float32),
        lax.psum_scatter(
            d_gain_mid.astype(jnp.bfloat16), "fsdp", scatter_dimension=0, tiled=True
        ).astype(jnp.float32),
        lax.psum_scatter(
            d_gain_query.astype(jnp.bfloat16), "fsdp", scatter_dimension=0, tiled=True
        ).astype(jnp.float32),
        lax.psum_scatter(
            d_gain_key.astype(jnp.bfloat16), "fsdp", scatter_dimension=0, tiled=True
        ).astype(jnp.float32),
        lax.psum_scatter(
            term_query.astype(jnp.bfloat16), "fsdp", scatter_dimension=0, tiled=True
        ).astype(jnp.float32),
        lax.psum_scatter(
            term_key.astype(jnp.bfloat16), "fsdp", scatter_dimension=0, tiled=True
        ).astype(jnp.float32),
        lax.psum_scatter(
            term_value.astype(jnp.bfloat16), "fsdp", scatter_dimension=0, tiled=True
        ).astype(jnp.float32),
        lax.psum_scatter(
            term_out.astype(jnp.bfloat16), "fsdp", scatter_dimension=0, tiled=True
        ).astype(jnp.float32),
    )
    summed = (
        lax.psum(grad_in.astype(jnp.bfloat16), "replica").astype(jnp.float32),
        lax.psum(grad_query.astype(jnp.bfloat16), "replica").astype(jnp.float32),
        lax.psum(grad_key.astype(jnp.bfloat16), "replica").astype(jnp.float32),
        lax.psum(grad_value.astype(jnp.bfloat16), "replica").astype(jnp.float32),
        lax.psum(grad_query_gain.astype(jnp.bfloat16), "replica").astype(jnp.float32),
        lax.psum(grad_key_gain.astype(jnp.bfloat16), "replica").astype(jnp.float32),
        lax.psum(grad_out.astype(jnp.bfloat16), "replica").astype(jnp.float32),
        lax.psum(grad_mid.astype(jnp.bfloat16), "replica").astype(jnp.float32),
        lax.psum(grad_gate.astype(jnp.bfloat16), "replica").astype(jnp.float32),
        lax.psum(grad_up.astype(jnp.bfloat16), "replica").astype(jnp.float32),
        lax.psum(grad_down.astype(jnp.bfloat16), "replica").astype(jnp.float32),
    )
    return (
        block_output,
        tokens_grad,
        summed[0],
        summed[1],
        summed[2],
        summed[3],
        summed[4],
        summed[5],
        summed[6],
        summed[7],
        summed[8],
        summed[9],
        summed[10],
    )


def solution(mesh):
    return jax.shard_map(
        on_device,
        mesh=mesh,
        in_specs=(
            P(("replica", "fsdp"), None),
            P("replica", None),
            P(("replica", "fsdp"), None),
            P("fsdp"),
            P("fsdp", None),
            P("fsdp", None),
            P("fsdp", None),
            P("fsdp"),
            P("fsdp"),
            P("fsdp", None),
            P("fsdp"),
            P(None, "fsdp"),
            P(None, "fsdp"),
            P("fsdp", None),
        ),
        out_specs=(
            P(("replica", "fsdp"), None),
            P(("replica", "fsdp"), None),
            P("fsdp"),
            P("fsdp", None),
            P("fsdp", None),
            P("fsdp", None),
            P("fsdp"),
            P("fsdp"),
            P("fsdp", None),
            P("fsdp"),
            P(None, "fsdp"),
            P(None, "fsdp"),
            P("fsdp", None),
        ),
        check_vma=False,
    )
```

profile of v0, /device:TPU:7, one launch (start us, length us, event | category | flops | bytes accessed | tf_op | source)
XLA Modules:
  0.0 1435.5 jit_solution(14032515137248771642)
XLA Ops:
  15.5 35.3 %all-reduce.13 = (bf16[1024]{0:T(1024)(128)(2,1)S(1)}, bf16[64]{0:T(256)(128)(2,1)S(1)}, bf16[64]{0:T(256)(128)(2,1)S(1)}, bf16[1024]{0:T(1024)(128)(2,1)S(1)}) all-reduce(bf16[1024]{0:T(1024)(128)(2,1)S(1)} %dynamic-update-slice, bf16[64]{0:T(256)(128)(2,1)S(1)} %dynamic-update-slice.1, ...), channel_id=1, replica_groups=mesh['replica'=8,'fsdp'=16] {'fsdp'}, use_global_device_ids=true, to_apply=%add.4 | all-reduce | flops 2176 | bytes 8704
  57.5 40.5 %all-gather.10.cloned.1.call-done = bf16[1024,512]{1,0:T(8,128)(2,1)} async-done(((bf16[64,512]{1,0:T(8,128)(2,1)}), bf16[1024,512]{1,0:T(8,128)(2,1)}) %all-gather.10.cloned.1.call-update) | async-done | bytes 1048592 | tf_op jit(solution)/shard_map/all_gather | solution.py:88
  104.0 41.2 %all-gather.18.cloned.1.call-done = bf16[1024,1024]{1,0:T(8,128)(2,1)} async-done(((bf16[64,1024]{1,0:T(8,128)(2,1)}), bf16[1024,1024]{1,0:T(8,128)(2,1)}) %all-gather.18.cloned.1.call-update) | async-done | bytes 2097168 | tf_op jit(solution)/shard_map/all_gather | solution.py:86
  148.6 46.4 %all-gather.16.cloned.1.call-done = bf16[2048,8,64]{0,2,1:T(8,128)(2,1)} async-done(((bf16[128,8,64]{0,2,1:T(8,128)(2,1)}), bf16[2048,8,64]{0,2,1:T(8,128)(2,1)}) %all-gather.16.cloned.1.call-update) | async-done | bytes 2097168 | tf_op jit(solution)/shard_map/all_gather | solution.py:111
  195.0 27.0 %while.45 = (s32[]{:T(128)}, f32[128,8,2]{0,2,1:T(2,128)S(1)}, f32[128,8,2]{0,2,1:T(2,128)S(1)}, s32[128]{0:T(128)S(1)}, s32[4]{0:T(128)}, /*index=5*/s32[2048]{...) while((s32[]{:T(128)}, f32[128,8,2]{0,2,1:T(2,128)S(1)}, ...), condition=%wide.region_13.14_spmd.clone, body=%wide.region_7.13_spmd.clone.sunk | while | flops 141824640 | bytes 9490227 | solution.py:145
  222.0 22.6 %all-gather.12.cloned.1.call-done = bf16[2048,8,64]{0,2,1:T(8,128)(2,1)} async-done(((bf16[128,8,64]{0,2,1:T(8,128)(2,1)}), bf16[2048,8,64]{0,2,1:T(8,128)(2,1)}) %all-gather.12.cloned.1.call-update) | async-done | bytes 2097168 | tf_op jit(solution)/shard_map/all_gather | solution.py:112
  244.7 27.0 %while.46 = (s32[]{:T(128)}, f32[128,8,2,64]{0,3,2,1:T(8,128)S(1)}, s32[128]{0:T(128)S(1)}, s32[4]{0:T(128)}, s32[2048]{0:T(1024)S(1)}, /*index=5*/bf16[2048,8,6...) while((s32[]{:T(128)}, f32[128,8,2,64]{0,3,2,1:T(8,128)S(1)}, ...), condition=%wide.region_18.19_spmd.clone, body=%wide.region_14.18_spmd.clone.sunk | while | flops 273023616 | bytes 2511647 | solution.py:169
  271.7 19.3 %all-gather.20.cloned.1.call-done = bf16[1024,1024]{1,0:T(8,128)(2,1)} async-done(((bf16[64,1024]{1,0:T(8,128)(2,1)}), bf16[1024,1024]{1,0:T(8,128)(2,1)}) %all-gather.20.cloned.1.call-update) | async-done | bytes 2097168 | tf_op jit(solution)/shard_map/all_gather | solution.py:89
  293.3 75.9 %all-gather.22.cloned.1.call-done = bf16[1024,4608]{0,1:T(8,128)(2,1)} async-done(((bf16[1024,288]{0,1:T(8,128)(2,1)}), bf16[1024,4608]{0,1:T(8,128)(2,1)}) %all-gather.22.cloned.1.call-update) | async-done | bytes 9437200 | tf_op jit(solution)/shard_map/all_gather | solution.py:176
  369.2 8.3 fusion.92
  377.6 69.2 %all-gather.24.cloned.1.call-done = bf16[1024,4608]{0,1:T(8,128)(2,1)} async-done(((bf16[1024,288]{0,1:T(8,128)(2,1)}), bf16[1024,4608]{0,1:T(8,128)(2,1)}) %all-gather.24.cloned.1.call-update) | async-done | bytes 9437200 | tf_op jit(solution)/shard_map/all_gather | solution.py:177
  446.7 8.3 fusion.93
  455.0 69.2 %all-gather.26.cloned.1.call-done = bf16[4608,1024]{1,0:T(8,128)(2,1)} async-done(((bf16[288,1024]{1,0:T(8,128)(2,1)}), bf16[4608,1024]{1,0:T(8,128)(2,1)}) %all-gather.26.cloned.1.call-update) | async-done | bytes 9437200 | tf_op jit(solution)/shard_map/all_gather | solution.py:178
  524.2 10.0 multiply_convert_fusion
  534.2 6.1 fusion.94
  547.2 36.4 %while.47 = (s32[]{:T(128)}, f32[128,8,2,64]{0,3,2,1:T(8,128)}, bf16[4,512,8,64]{1,3,2,0:T(8,128)(2,1)}, bf16[4,512,8,64]{1,3,2,0:T(8,128)(2,1)}, s32[128]{0:T(1...) while((s32[]{:T(128)}, f32[128,8,2,64]{0,3,2,1:T(8,128)}, ...), condition=%wide.region_26.27_spmd.clone, body=%wide.region_22.26_spmd.clone.sunk | while | flops 682623616 | bytes 30183900 | solution.py:255
  552.9 9.7 conditional.11
  589.3 6.5 reshape.288
  601.5 6.5 reshape.290
  614.0 82.9 %reduce-scatter.28.cloned.1.call-done = bf16[128,512]{1,0:T(8,128)(2,1)} async-done(((bf16[2048,512]{1,0:T(8,128)(2,1)}), bf16[128,512]{1,0:T(8,128)(2,1)}) %reduce-scatter.28.cloned.1.call-update) | async-done | bytes 131088
  700.0 74.4 %reduce-scatter.30.cloned.1.call-done = bf16[128,512]{1,0:T(8,128)(2,1)} async-done(((bf16[2048,512]{1,0:T(8,128)(2,1)}), bf16[128,512]{1,0:T(8,128)(2,1)}) %reduce-scatter.30.cloned.1.call-update) | async-done | bytes 131088 | tf_op jit(solution)/shard_map/convert_element_type | solution.py:278
  796.4 5.9 fusion.61
  802.4 48.9 %reduce-scatter.14.cloned.1.call-done = bf16[64,1024]{1,0:T(8,128)(2,1)} async-done(((bf16[1024,1024]{1,0:T(8,128)(2,1)}), bf16[64,1024]{1,0:T(8,128)(2,1)}) %reduce-scatter.14.cloned.1.call-update) | async-done | bytes 131088 | tf_op jit(solution)/shard_map/reduce_scatter | solution.py:310
  851.3 77.3 %reduce-scatter.20.cloned.1.call-done = bf16[64,1024]{1,0:T(8,128)(2,1)} async-done(((bf16[1024,1024]{1,0:T(8,128)(2,1)}), bf16[64,1024]{1,0:T(8,128)(2,1)}) %reduce-scatter.20.cloned.1.call-update) | async-done | bytes 131088 | tf_op jit(solution)/shard_map/reduce_scatter | solution.py:319
  928.6 75.4 %reduce-scatter.16.cloned.1.call-done = bf16[64,512]{1,0:T(8,128)(2,1)} async-done(((bf16[1024,512]{1,0:T(8,128)(2,1)}), bf16[64,512]{1,0:T(8,128)(2,1)}) %reduce-scatter.16.cloned.1.call-update) | async-done | bytes 65552 | tf_op jit(solution)/shard_map/reduce_scatter | solution.py:313
  1004.0 75.7 %reduce-scatter.18.cloned.1.call-done = bf16[64,512]{1,0:T(8,128)(2,1)} async-done(((bf16[1024,512]{1,0:T(8,128)(2,1)}), bf16[64,512]{1,0:T(8,128)(2,1)}) %reduce-scatter.18.cloned.1.call-update) | async-done | bytes 65552 | tf_op jit(solution)/shard_map/reduce_scatter | solution.py:316
  1079.7 91.0 %reduce-scatter.22.cloned.1.call-done = bf16[1024,288]{0,1:T(8,128)(2,1)} async-done(((bf16[1024,4608]{0,1:T(8,128)(2,1)}), bf16[1024,288]{0,1:T(8,128)(2,1)}) %reduce-scatter.22.cloned.1.call-update) | async-done | bytes 589840 | tf_op jit(solution)/shard_map/reduce_scatter | solution.py:194
  1170.6 90.2 %reduce-scatter.24.cloned.1.call-done = bf16[1024,288]{0,1:T(8,128)(2,1)} async-done(((bf16[1024,4608]{0,1:T(8,128)(2,1)}), bf16[1024,288]{0,1:T(8,128)(2,1)}) %reduce-scatter.24.cloned.1.call-update) | async-done | bytes 589840 | tf_op jit(solution)/shard_map/reduce_scatter | solution.py:197
  1260.9 90.1 %reduce-scatter.26.cloned.1.call-done = bf16[288,1024]{1,0:T(8,128)(2,1)} async-done(((bf16[4608,1024]{1,0:T(8,128)(2,1)}), bf16[288,1024]{1,0:T(8,128)(2,1)}) %reduce-scatter.26.cloned.1.call-update) | async-done | bytes 589840 | tf_op jit(solution)/shard_map/reduce_scatter | solution.py:200
  1353.4 31.4 %all-reduce.12 = (bf16[1024]{0:T(1024)(128)(2,1)S(1)}, bf16[64]{0:T(256)(128)(2,1)S(1)}, bf16[64]{0:T(256)(128)(2,1)S(1)}, bf16[1024]{0:T(1024)(128)(2,1)S(1)}) all-reduce(bf16[1024]{0:T(1024)(128)(2,1)S(1)} %get-tuple-element.391, bf16[64]{0:T(256)(128)(2,1)S(1)} %get-tuple-element.393, ...), channel_id=4, replica_groups=mesh['replica'=8,'fsdp'=16] {'fsdp'}, use_global_device_ids=true, to_apply=%region_33.34.clone | all-reduce | flops 2176 | bytes 8704
  1385.1 18.7 %all-reduce.14 = (bf16[64]{0:T(256)(128)(2,1)S(1)}, bf16[4]{0:T(256)(128)(2,1)S(1)}, bf16[4]{0:T(256)(128)(2,1)S(1)}, bf16[64]{0:T(256)(128)(2,1)S(1)}) all-reduce(bf16[64]{0:T(256)(128)(2,1)S(1)} %dynamic-slice.5, bf16[4]{0:T(256)(128)(2,1)S(1)} %dynamic-slice.7, ...), channel_id=1, replica_groups=mesh['replica'=8,'fsdp'=16] {'replica'}, use_global_device_ids=true, to_apply=%region_34.35 | all-reduce | flops 136 | bytes 544 | tf_op jit(solution)/shard_map/psum | solution.py:324
  1406.9 13.2 all-reduce.18.cloned.1.call-done
  (319 shorter events, 149.8 us)
Async XLA Ops:
  7.2 90.9 %copy-start.1 = (bf16[128,1024]{1,0:T(8,128)(2,1)S(1)}, bf16[128,1024]{1,0:T(8,128)(2,1)}, u32[]{:S(2)}) copy-start(bf16[128,1024]{1,0:T(8,128)(2,1)} %param.26) | copy-start | bytes 786436
  7.2 46.8 %all-gather.14.cloned.1.call-start = ((), (), s32[]{:S(2)}) async-start(), calls=%async_computation.11 | async-start | bytes 1114112 | tf_op jit(solution)/shard_map/all_gather | solution.py:87
  7.9 90.1 %all-gather.10.cloned.1.call-start = ((), (), s32[]{:S(2)}) async-start(), calls=%async_computation.9 | async-start | bytes 1114112 | tf_op jit(solution)/shard_map/all_gather | solution.py:88
  8.7 136.5 %all-gather.18.cloned.1.call-start = ((), (), s32[]{:S(2)}) async-start(), calls=%async_computation.13 | async-start | bytes 2228224 | tf_op jit(solution)/shard_map/all_gather | solution.py:86
  9.4 185.6 %all-gather.16.cloned.1.call-start = ((), (), s32[]{:S(2)}) async-start(), calls=%async_computation.12 | async-start | bytes 2228224 | tf_op jit(solution)/shard_map/all_gather | solution.py:111
  50.8 49.6 %copy-start.41 = (f32[64]{0:T(128)}, f32[64]{0:T(128)S(1)}, u32[]{:S(2)}) copy-start(f32[64]{0:T(128)S(1)} %convert_element_type.214) | copy-start | bytes 772
  53.5 46.9 %copy-start.43 = (f32[128]{0:T(128)}, f32[128]{0:T(128)S(1)}, u32[]{:S(2)}) copy-start(f32[128]{0:T(128)S(1)} %fusion.69) | copy-start | bytes 1540
  57.5 187.2 %all-gather.12.cloned.1.call-start = ((), (), s32[]{:S(2)}) async-start(), calls=%async_computation.10 | async-start | bytes 2228224 | tf_op jit(solution)/shard_map/all_gather | solution.py:112
  100.4 190.6 %all-gather.20.cloned.1.call-start = ((), (), s32[]{:S(2)}) async-start(), calls=%async_computation.14 | async-start | bytes 2228224 | tf_op jit(solution)/shard_map/all_gather | solution.py:89
  101.0 268.2 %all-gather.22.cloned.1.call-start = ((), (), s32[]{:S(2)}) async-start(), calls=%async_computation.15 | async-start | bytes 10027008 | tf_op jit(solution)/shard_map/all_gather | solution.py:176
  101.8 345.0 %all-gather.24.cloned.1.call-start = ((), (), s32[]{:S(2)}) async-start(), calls=%async_computation.16 | async-start | bytes 10027008 | tf_op jit(solution)/shard_map/all_gather | solution.py:177
  102.5 421.7 %all-gather.26.cloned.1.call-start = ((), (), s32[]{:S(2)}) async-start(), calls=%async_computation.17 | async-start | bytes 10027008 | tf_op jit(solution)/shard_map/all_gather | solution.py:178
  103.3 593.7 %reduce-scatter.28.cloned.1.call-start = ((), (), s32[]{:S(2)}) async-start(), calls=%async_computation.25 | async-start | bytes 2228224
  271.7 105.9 %copy-start.25 = (bf16[128,8,2,64]{0,3,2,1:T(8,128)(2,1)}, bf16[128,8,2,64]{0,3,2,1:T(8,128)(2,1)S(1)}, u32[]{:S(2)}) copy-start(bf16[128,8,2,64]{0,3,2,1:T(8,128)(2,1)S(1)} %convert_element_type.217) | copy-start | bytes 786436
  293.2 248.9 %copy-start.6 = (f32[128,1024]{1,0:T(8,128)}, f32[128,1024]{1,0:T(8,128)S(1)}, u32[]{:S(2)}) copy-start(f32[128,1024]{1,0:T(8,128)S(1)} %get-tuple-element.514) | copy-start | bytes 1572868
  293.3 153.4 %copy-start.19 = (bf16[128,1024]{1,0:T(8,128)(2,1)}, bf16[128,1024]{1,0:T(8,128)(2,1)S(1)}, u32[]{:S(2)}) copy-start(bf16[128,1024]{1,0:T(8,128)(2,1)S(1)} %multiply_convert_fusion.2) | copy-start | bytes 786436
  377.6 146.7 %copy-start.28 = (bf16[128,1024]{1,0:T(8,128)(2,1)S(1)}, bf16[128,1024]{1,0:T(8,128)(2,1)}, u32[]{:S(2)}) copy-start(bf16[128,1024]{1,0:T(8,128)(2,1)} %param.28) | copy-start | bytes 786436
  595.7 178.6 %reduce-scatter.30.cloned.1.call-start = ((), (), s32[]{:S(2)}) async-start(), calls=%async_computation.26 | async-start | bytes 2228224 | tf_op jit(solution)/shard_map/convert_element_type | solution.py:278
  608.0 243.3 %reduce-scatter.14.cloned.1.call-start = ((), (), s32[]{:S(2)}) async-start(), calls=%async_computation.18 | async-start | bytes 2228224 | tf_op jit(solution)/shard_map/reduce_scatter | solution.py:310
  611.8 316.8 %reduce-scatter.20.cloned.1.call-start = ((), (), s32[]{:S(2)}) async-start(), calls=%async_computation.21 | async-start | bytes 2228224 | tf_op jit(solution)/shard_map/reduce_scatter | solution.py:319
  614.0 84.1 %copy-start.22 = (f32[128,512]{0,1:T(8,128)S(1)}, f32[128,512]{0,1:T(8,128)}, u32[]{:S(2)}) copy-start(f32[128,512]{0,1:T(8,128)} %copy-done.21) | copy-start | bytes 786436
  614.0 84.1 %copy-start.42 = (f32[64]{0:T(128)S(1)}, f32[64]{0:T(128)}, u32[]{:S(2)}) copy-start(f32[64]{0:T(128)} %copy-done.41) | copy-start | bytes 772
  614.0 390.0 %reduce-scatter.16.cloned.1.call-start = ((), (), s32[]{:S(2)}) async-start(), calls=%async_computation.19 | async-start | bytes 1114112 | tf_op jit(solution)/shard_map/reduce_scatter | solution.py:313
  698.4 78.5 %copy-start.16 = (bf16[128,4608]{1,0:T(8,128)(2,1)S(1)}, bf16[128,4608]{1,0:T(8,128)(2,1)}, u32[]{:S(2)}) copy-start(bf16[128,4608]{1,0:T(8,128)(2,1)} %copy-done.15) | copy-start | bytes 3538948
  698.4 78.5 %copy-start.20 = (bf16[128,1024]{1,0:T(8,128)(2,1)S(1)}, bf16[128,1024]{1,0:T(8,128)(2,1)}, u32[]{:S(2)}) copy-start(bf16[128,1024]{1,0:T(8,128)(2,1)} %copy-done.19) | copy-start | bytes 786436
  699.9 379.8 %reduce-scatter.18.cloned.1.call-start = ((), (), s32[]{:S(2)}) async-start(), calls=%async_computation.20 | async-start | bytes 1114112 | tf_op jit(solution)/shard_map/reduce_scatter | solution.py:316
  776.8 393.8 %reduce-scatter.22.cloned.1.call-start = ((), (), s32[]{:S(2)}) async-start(), calls=%async_computation.22 | async-start | bytes 10027008 | tf_op jit(solution)/shard_map/reduce_scatter | solution.py:194
  782.2 478.7 %reduce-scatter.24.cloned.1.call-start = ((), (), s32[]{:S(2)}) async-start(), calls=%async_computation.23 | async-start | bytes 10027008 | tf_op jit(solution)/shard_map/reduce_scatter | solution.py:197
  788.7 562.4 %reduce-scatter.26.cloned.1.call-start = ((), (), s32[]{:S(2)}) async-start(), calls=%async_computation.24 | async-start | bytes 10027008 | tf_op jit(solution)/shard_map/reduce_scatter | solution.py:200
  795.1 625.0 %all-reduce.18.cloned.1.call-start = ((), (), s32[]{:S(2)}) async-start(), calls=%async_computation.27 | async-start | bytes 4325376 | tf_op jit(solution)/shard_map/psum | solution.py:325
  802.4 548.7 %copy-start.11 = (bf16[1024,1024]{1,0:T(8,128)(2,1)S(1)}, bf16[1024,1024]{1,0:T(8,128)(2,1)}, u32[]{:S(2)}) copy-start(bf16[1024,1024]{1,0:T(8,128)(2,1)} %all-gather.18.cloned.1.call-done) | copy-start | bytes 6291460
  1352.3 53.6 %copy-start.44 = (f32[128]{0:T(128)S(1)}, f32[128]{0:T(128)}, u32[]{:S(2)}) copy-start(f32[128]{0:T(128)} %copy-done.43) | copy-start | bytes 1540
  (35 other events, 177.6 us)
Sparse Core Ops, SparseCore 0:
  10.2 43.7 all-gather.13
  56.1 41.8 all-gather.9
  100.2 44.9 all-gather.17
  147.7 47.2 all-gather.15
  197.5 47.0 all-gather.11
  246.6 44.3 all-gather.19
  293.2 75.9 all-gather.21
  371.4 75.2 all-gather.23
  448.9 75.2 all-gather.25
  595.9 101.0 reduce-scatter.27
  700.6 73.7 reduce-scatter.29
  777.5 73.7 reduce-scatter.13
  854.9 73.6 reduce-scatter.19
  931.7 72.2 reduce-scatter.15
  1007.3 72.2 reduce-scatter.17
  1083.0 87.5 reduce-scatter.21
  1174.4 86.4 reduce-scatter.23
  1264.2 86.7 reduce-scatter.25
  1354.1 65.8 all-reduce.17
where the time goes:
time: 1440 us
  waiting for transfers between devices  1110 us (77%)
  matrix products  87.7 us (6%)
  blocking collectives  85.4 us (6%)
  local copies, waits for them, and re-layouts  59.6 us (4%)
  loops' own time  38.1 us (3%)
  other arithmetic  37.4 us (3%)
  between operations  17.7 us (1%)
    reduce_scatter x1, waiting for transfers between devices, on_device(): lax.psum_scatter(term_gate.astype(jnp.bfloat16), 'fsdp', scatter_dimensio...  91 us
    reduce_scatter x1, waiting for transfers between devices, on_device(): lax.psum_scatter(term_up.astype(jnp.bfloat16), 'fsdp', scatter_dimension=...  90.2 us
    reduce_scatter x1, waiting for transfers between devices, on_device(): lax.psum_scatter(term_down.astype(jnp.bfloat16), 'fsdp', scatter_dimensio...  90.1 us
    unnamed x20, waiting for transfers between devices  87.8 us
    reduce_scatter x1, waiting for transfers between devices, on_device(): lax.psum_scatter(term_out.astype(jnp.bfloat16), 'fsdp', scatter_dimension...  77.3 us
    all_gather x1, waiting for transfers between devices, on_device(): lax.all_gather(gate_weight, 'fsdp', axis=1, tiled=True)  75.9 us
    reduce_scatter x1, waiting for transfers between devices, on_device(): lax.psum_scatter(term_value.astype(jnp.bfloat16), 'fsdp', scatter_dimensi...  75.7 us
    reduce_scatter x1, waiting for transfers between devices, on_device(): lax.psum_scatter(term_key.astype(jnp.bfloat16), 'fsdp', scatter_dimension...  75.4 us
  transfers between devices with their start and end apart: 19, of which 19 were waited for; matrix products, arithmetic and copies ran while one was open for 8% of the time, Pallas kernels for 0%

commit v1 on v0

v1 whole, which is shorter than its diff:
```python
import functools

import jax
import jax.numpy as jnp
import numpy as np
from jax import lax
from jax.experimental import pallas as pl
from jax.experimental.pallas import tpu as pltpu
from jax.sharding import PartitionSpec as P

F32 = jnp.float32
BF16 = jnp.bfloat16
EPS = 1e-05
ROPE_BASE = 1000000.0
HEAD_DIM = 64


def shape(dims, dtype):
    return jax.ShapeDtypeStruct(dims, dtype)


def run(kernel, outs, args, scratch=()):
    at, rest = args[0], args[1:]
    return pl.pallas_call(
        kernel,
        out_shape=[shape(dims, dtype) for dims, dtype in outs],
        in_specs=[pl.BlockSpec(memory_space=pltpu.SMEM)]
        + [pl.BlockSpec(memory_space=pltpu.VMEM)] * len(rest),
        out_specs=[pl.BlockSpec(memory_space=pltpu.VMEM)] * len(outs),
        scratch_shapes=list(scratch),
        compiler_params=pltpu.CompilerParams(vmem_limit_bytes=50 * 1024 * 1024),
    )(at, *rest)


def yz_perm(dy, dz):
    return [
        (y * 4 + z, ((y + dy) % 4) * 4 + (z + dz) % 4) for y in range(4) for z in range(4)
    ]


def to_y(value, step):
    return lax.ppermute(value, "fsdp", yz_perm(step, 0))


def to_z(value, step):
    return lax.ppermute(value, "fsdp", yz_perm(0, step))


def to_x(value, step):
    pairs = [(x * 2 + c, ((x + step) % 4) * 2 + c) for x in range(4) for c in range(2)]
    return lax.ppermute(value, "replica", pairs)


def to_core(value):
    return lax.ppermute(value, "replica", [(i, i ^ 1) for i in range(8)])


def gather(move, own):
    return [own] + [move(own, step) for step in (1, 2, 3)]


def scatter(move, blocks):
    return [blocks[0]] + [move(blocks[step], -step) for step in (1, 2, 3)]


def back(place, step):
    return lax.rem(place - step + 4, 4)


def ahead(place, step):
    return lax.rem(place + step, 4)


def rows_at(start, count):
    return pl.ds(pl.multiple_of(start, count), count)


def nt(left, right):
    return lax.dot_general(left, right, (((1,), (1,)), ((), ())), preferred_element_type=F32)


def nn(left, right):
    return jnp.dot(left, right, preferred_element_type=F32)


def lane_of(value):
    return lax.broadcasted_iota(jnp.int32, value.shape, value.ndim - 1)


def low_lanes(value):
    return lane_of(value) < HEAD_DIM


def swap_halves(value):
    first = lax.rem(lane_of(value), HEAD_DIM) < HEAD_DIM // 2
    return jnp.where(first, pltpu.roll(value, 96, 1), pltpu.roll(value, 32, 1))


def head_mean(value):
    low = low_lanes(value)
    left = jnp.sum(jnp.where(low, value, 0.0), axis=1, keepdims=True)
    right = jnp.sum(jnp.where(low, 0.0, value), axis=1, keepdims=True)
    return jnp.where(low, left, right) * (1.0 / HEAD_DIM)


def head_forward(raw, gain, cosine, sine):
    normed = raw * lax.rsqrt(head_mean(raw * raw) + EPS) * gain
    return normed * cosine + swap_halves(normed) * sine


def head_backward(grad, raw, gain, cosine, sine):
    turned = grad * cosine - swap_halves(grad) * sine
    scale = lax.rsqrt(head_mean(raw * raw) + EPS)
    scaled = turned * gain
    d_raw = scale * scaled - raw * (scale * scale * scale) * head_mean(scaled * raw)
    return d_raw, jnp.sum(turned * raw * scale, axis=0, keepdims=True)


def gain_rows(tile):
    row = tile[0:8, :]
    turned = pltpu.roll(row, 64, 1)
    low = low_lanes(row)
    return jnp.where(low, row, turned)[0:1], jnp.where(low, turned, row)[0:1]


def middle_gain_row(tile):
    return jnp.concatenate([tile[8 + i : 9 + i, :] for i in range(8)], axis=1)


def stack_heads(tile, group):
    low = low_lanes(tile)
    turned = pltpu.roll(tile, 64, 1)
    if group == 0:
        pair = [jnp.where(low, tile, 0.0), jnp.where(low, turned, 0.0)]
    else:
        pair = [jnp.where(low, 0.0, turned), jnp.where(low, 0.0, tile)]
    return jnp.concatenate(pair, axis=0).astype(BF16)


def unstack_heads(stacked, group):
    top, bottom = stacked[0:128], stacked[128:256]
    low = low_lanes(top)
    if group == 0:
        return jnp.where(low, top, pltpu.roll(bottom, 64, 1))
    return jnp.where(low, pltpu.roll(top, 64, 1), bottom)


def visible_part(part, starts, place, last):
    key_place = lax.broadcasted_iota(jnp.int32, (512, 256), 0) + part * 512
    seen = key_place >= starts
    return seen & (key_place <= place) if last else seen


def row_places(block, z, starts_ref):
    place = (4 * block + z) * 128 + lax.broadcasted_iota(jnp.int32, (1, 128), 1)
    start = starts_ref[block : block + 1, :]
    return jnp.concatenate([place, place], axis=1), jnp.concatenate([start, start], axis=1)


def prepare(at, gains, rows, w_q, w_k, w_v, normed, *sends):
    y, z = at[0], at[1]
    place = 4 * y + z
    source = rows[...].astype(F32)
    scale = lax.rsqrt(jnp.mean(source * source, axis=1, keepdims=True) + EPS)
    normed[...] = (source * scale).astype(BF16)
    held = gains[...]
    lane = lax.broadcasted_iota(jnp.int32, (64, 128), 1)
    line = lax.broadcasted_iota(jnp.int32, (64, 128), 0)
    column = jnp.sum(jnp.where(lane == line, held[0:1, :], 0.0), axis=1, keepdims=True)
    heads = pltpu.roll(held, 4 * place, 1)[2:3] + pltpu.roll(held, 64 + 4 * place, 1)[3:4]
    middle = pltpu.roll(held, 64 * lax.rem(place, 2), 1)[1:2]
    line = lax.broadcasted_iota(jnp.int32, (16, 128), 0)
    tile = jnp.where(line == 0, heads, 0.0) + jnp.where(line == 8 + place // 2, middle, 0.0)
    for step in range(4):
        other = ahead(y, step)
        send = sends[step]
        for source_ref, width, first in ((w_q, 256, 0), (w_k, 128, 256), (w_v, 128, 384)):
            block = source_ref[:, rows_at(other * width, width)].astype(F32) * column
            send[0:64, first : first + width] = block.astype(BF16)
        send[64:80, 0:128] = tile.astype(BF16)
        send[64:80, 128:512] = jnp.zeros((16, 384), BF16)


def project(at, *refs):
    x_parts, w_parts = refs[0:4], refs[4:8]
    cosine_ref, sine_ref = refs[8:10]
    query, key_value, raw, x_full, w_full, gain_tile = refs[10:]
    y, z = at[0], at[1]
    total = jnp.zeros((16, 128), F32)
    for step in range(4):
        x_full[rows_at(back(y, step) * 128, 128), :] = x_parts[step][...]
        for inner in range(4):
            place = back(y, inner) * 4 + back(z, step)
            first = inner * 80
            w_full[rows_at(place * 64, 64), :] = w_parts[step][first : first + 64, :]
            total = total + w_parts[step][first + 64 : first + 80, 0:128].astype(F32)
    gain_tile[...] = total
    gain_q, gain_k = gain_rows(total)
    cosine, sine = cosine_ref[...], sine_ref[...]
    product = nn(x_full[...], w_full[...])
    raw[...] = product[:, 0:384]
    for tile in range(2):
        part = product[:, tile * 128 : tile * 128 + 128]
        turned = head_forward(part, gain_q, cosine, sine) * (HEAD_DIM**-0.5)
        query[:, tile * 128 : tile * 128 + 128] = turned.astype(BF16)
    key_value[:, 0:128] = head_forward(product[:, 256:384], gain_k, cosine, sine).astype(BF16)
    key_value[:, 128:256] = product[:, 384:512].astype(BF16)


def attend(at, query, *refs):
    kv_parts, out_parts, starts = refs[0:4], refs[4:8], refs[8]
    keys, values, attended, inverse, w_out = refs[9:14]
    partials, (values_t, mixed) = refs[14:18], refs[18:]
    y, z = at[0], at[1]
    for step in range(4):
        other = back(z, step)
        for block in range(4):
            rows = kv_parts[step][block * 128 : block * 128 + 128, :]
            target = rows_at((4 * block + other) * 128, 128)
            keys[target, :] = rows[:, 0:128]
            values[target, :] = rows[:, 128:256]
        w_out[rows_at(other * 64, 64), :] = out_parts[step][...]
    for part in range(4):
        chunk = values[part * 512 : part * 512 + 512, :].astype(F32)
        values_t[:, part * 512 : part * 512 + 512] = chunk.T.astype(BF16)
    for block in range(4):
        place, start = row_places(block, z, starts)
        rows = slice(block * 128, block * 128 + 128)
        for group in range(2):
            lanes = slice(group * 128, group * 128 + 128)
            stacked = stack_heads(query[rows, lanes].astype(F32), group)
            total = jnp.zeros((1, 256), F32)
            mix = jnp.zeros((128, 256), F32)
            for part in range(block + 1):
                span = slice(part * 512, part * 512 + 512)
                scores = nt(keys[span, :], stacked)
                seen = visible_part(part, start, place, part == block)
                weights = jnp.where(seen, jnp.exp(scores), 0.0)
                total = total + jnp.sum(weights, axis=0, keepdims=True)
                mix = mix + nn(values_t[:, span], weights.astype(BF16))
            share = 1.0 / total
            inverse[block * 2 + group : block * 2 + group + 1, :] = share
            attended[rows, lanes] = unstack_heads((mix * share).T, group).astype(BF16)
    mixed[...] = nn(attended[...], w_out[...])
    for step in range(4):
        partials[step][...] = mixed[rows_at(back(y, step) * 128, 128), :].astype(BF16)


def sum_parts(parts):
    total = parts[0][...].astype(F32)
    for part in parts[1:]:
        total = total + part[...].astype(F32)
    return total


def join_middle(at, rows, gain_tile, *refs):
    parts, (middle, normed) = refs[0:4], refs[4:]
    total = rows[...].astype(F32) + sum_parts(parts)
    middle[...] = total
    scale = lax.rsqrt(jnp.mean(total * total, axis=1, keepdims=True) + EPS)
    normed[...] = (total * scale * middle_gain_row(gain_tile[...])).astype(BF16)


def back_middle(at, middle, cotangent, gain_tile, *refs):
    parts, (d_middle, d_low, gain_grad) = refs[0:4], refs[4:]
    grad = sum_parts(parts)
    source = middle[...]
    scale = lax.rsqrt(jnp.mean(source * source, axis=1, keepdims=True) + EPS)
    scaled = grad * middle_gain_row(gain_tile[...])
    share = jnp.mean(scaled * source, axis=1, keepdims=True)
    total = cotangent[...].astype(F32) + scale * scaled - source * (scale**3 * share)
    d_middle[...] = total
    d_low[...] = total.astype(BF16)
    line = jnp.sum(grad * source * scale, axis=0, keepdims=True)
    gain_grad[...] = jnp.broadcast_to(line, (8, 1024))


def attend_back(at, query, keys, values, attended, inverse, w_out, starts, *refs):
    d_parts, (raw, cosine_ref, sine_ref, gain_tile) = refs[0:4], refs[4:8]
    d_kv, (d_query, gain_grad, out_grad) = refs[8:12], refs[12:15]
    d_rows, d_keys, d_values, keys_t, d_mixed = refs[15:]
    y, z = at[0], at[1]
    for step in range(4):
        d_rows[rows_at(back(y, step) * 128, 128), :] = d_parts[step][...]
    d_mixed[...] = nt(d_rows[...], w_out[...]).astype(BF16).astype(F32)
    for part in range(4):
        span = slice(part * 512, part * 512 + 512)
        keys_t[:, span] = keys[span, :].astype(F32).T.astype(BF16)
    d_keys[...] = jnp.zeros((2048, 128), F32)
    d_values[...] = jnp.zeros((2048, 128), F32)
    gain_q, _ = gain_rows(gain_tile[...])
    line = jnp.zeros((1, 128), F32)
    for block in range(4):
        place, start = row_places(block, z, starts)
        rows = slice(block * 128, block * 128 + 128)
        for group in range(2):
            lanes = slice(group * 128, group * 128 + 128)
            stacked = stack_heads(query[rows, lanes].astype(F32), group)
            d_tile = d_mixed[rows, lanes]
            d_stacked = stack_heads(d_tile, group)
            product = (d_tile * attended[rows, lanes].astype(F32)).T
            delta = jnp.concatenate(
                [
                    jnp.sum(product[0:64], axis=0, keepdims=True),
                    jnp.sum(product[64:128], axis=0, keepdims=True),
                ],
                axis=1,
            )
            share = inverse[block * 2 + group : block * 2 + group + 1, :]
            d_turned = jnp.zeros((128, 256), F32)
            for part in range(block + 1):
                span = slice(part * 512, part * 512 + 512)
                scores = nt(keys[span, :], stacked)
                seen = visible_part(part, start, place, part == block)
                probs = jnp.where(seen, jnp.exp(scores) * share, 0.0)
                d_probs = nt(values[span, :], d_stacked)
                d_scores = (probs * (d_probs - delta)).astype(BF16)
                d_values[span, :] += nn(probs.astype(BF16), d_stacked)
                d_keys[span, :] += nn(d_scores, stacked)
                d_turned = d_turned + nn(keys_t[:, span], d_scores)
            d_head = unstack_heads(d_turned.T, group) * (HEAD_DIM**-0.5)
            d_raw, gain_part = head_backward(
                d_head, raw[rows, lanes], gain_q, cosine_ref[rows, :], sine_ref[rows, :]
            )
            d_query[rows, lanes] = d_raw.astype(BF16)
            line = line + gain_part
    for step in range(4):
        other = back(z, step)
        for block in range(4):
            source = rows_at((4 * block + other) * 128, 128)
            rows = slice(block * 128, block * 128 + 128)
            d_kv[step][rows, 0:128] = d_keys[source, :].astype(BF16)
            d_kv[step][rows, 128:256] = d_values[source, :].astype(BF16)
    wide = jnp.broadcast_to(line, (8, 128))
    gain_grad[...] = wide + pltpu.roll(wide, 64, 1)
    out_grad[...] = nn(attended[...].astype(F32).T.astype(BF16), d_rows[...])


def weight_back(at, raw, cosine, sine, gain_tile, d_query, query_gain, middle_gain, *refs):
    parts, (x_full, out_grad) = refs[0:4], refs[4:6]
    d_joint, keep, send = refs[6:9]
    grads, extras = refs[9:]
    z, core = at[1], at[3]
    total = sum_parts(parts)
    _, gain_k = gain_rows(gain_tile[...])
    d_key, key_line = head_backward(
        total[:, 0:128], raw[:, 256:384], gain_k, cosine[...], sine[...]
    )
    d_joint[:, 0:256] = d_query[...]
    d_joint[:, 256:384] = d_key.astype(BF16)
    d_joint[:, 384:512] = total[:, 128:256].astype(BF16)
    wide = jnp.broadcast_to(key_line, (8, 128))
    wide = wide + pltpu.roll(wide, 64, 1)
    line = lax.broadcasted_iota(jnp.int32, (16, 128), 0)
    heads_q = jnp.concatenate([query_gain[...], query_gain[...]], axis=0)
    heads_k = jnp.concatenate([wide, wide], axis=0)
    for place in range(16):
        half = middle_gain[0:8, (place // 2) * 128 : (place // 2) * 128 + 128]
        half = jnp.concatenate([half, half], axis=0)
        if place % 2:
            half = pltpu.roll(half, 64, 1)
        turn = (128 - 4 * place) % 128
        tile = jnp.where(line == 0, half, 0.0)
        tile = tile + jnp.where(line == 1, pltpu.roll(heads_q, turn, 1) if turn else heads_q, 0.0)
        tile = tile + jnp.where(line == 2, pltpu.roll(heads_k, turn, 1) if turn else heads_k, 0.0)
        extras[place * 16 : place * 16 + 16, :] = tile
    grads[...] = lax.dot_general(
        x_full[...], d_joint[...], (((0,), (0,)), ((), ())), preferred_element_type=F32
    )
    for target, which in ((send, 1 - core), (keep, core)):
        for step in range(4):
            other = back(z, step)
            for block in range(4):
                place = block * 4 + other
                first = block * 80
                target[step, first : first + 64, :] = grads[
                    rows_at(place * 64, 64), rows_at(which * 256, 256)
                ].astype(BF16)
                target[step, first + 64 : first + 80, 0:128] = extras[
                    rows_at(place * 16, 16), :
                ].astype(BF16)
                target[step, first + 64 : first + 80, 128:256] = jnp.zeros((16, 128), BF16)
            for column in range(2):
                first = 320 + 64 * column
                target[step, first : first + 64, :] = out_grad[
                    rows_at(other * 64, 64), rows_at(which * 512 + column * 256, 256)
                ].astype(BF16)


def input_back(at, d_joint, w_full, *refs):
    blocks, (total,) = refs[0:4], refs[4:]
    y = at[0]
    total[...] = nt(d_joint[...], w_full[...])
    for step in range(4):
        blocks[step][...] = total[rows_at(back(y, step) * 128, 128), :].astype(BF16)


def join_tokens(at, rows, d_middle, *refs):
    parts, (out,) = refs[0:4], refs[4:]
    grad = sum_parts(parts)
    source = rows[...].astype(F32)
    scale = lax.rsqrt(jnp.mean(source * source, axis=1, keepdims=True) + EPS)
    share = jnp.mean(grad * source, axis=1, keepdims=True)
    out[...] = d_middle[...] + scale * grad - source * (scale**3 * share)


def tail_core(at, keep, received, *outs):
    for step in range(4):
        outs[step][...] = (keep[step].astype(F32) + received[step].astype(F32)).astype(BF16)


def tail_z(at, *refs):
    parts, blocks, out_rows, total = refs[0:4], refs[4:8], refs[8], refs[9]
    y = at[0]
    total[...] = sum_parts(parts)
    for step in range(4):
        blocks[step][...] = total[rows_at(back(y, step) * 80, 80), :].astype(BF16)
    out_rows[...] = total[320:448, :].astype(BF16)


def tail_x(at, own, one, two, three, out):
    even = own[...].astype(F32) + two[...].astype(F32)
    odd = one[...].astype(F32) + three[...].astype(F32)
    out[...] = (even + odd).astype(BF16)


def tail_out(at, own, other, gains, w_q, w_k, w_v, g_q, g_k, g_v, g_out, g_gain):
    y, core = at[0], at[3]
    own_low = core == 0
    first = jnp.where(own_low, own[...].astype(F32), other[...].astype(F32))
    second = jnp.where(own_low, other[...].astype(F32), own[...].astype(F32))
    lane = lax.broadcasted_iota(jnp.int32, (64, 128), 1)
    line = lax.broadcasted_iota(jnp.int32, (64, 128), 0)
    column = jnp.sum(jnp.where(lane == line, gains[0:1, :], 0.0), axis=1, keepdims=True)
    products = jnp.zeros((64, 128), F32)
    extra = jnp.zeros((16, 128), F32)
    for step in range(4):
        group = ahead(y, step)
        top = step * 80
        extra = extra + first[top + 64 : top + 80, 0:128]
        for source, left, width, weight, grad in (
            (first, 0, 256, w_q, g_q),
            (second, 0, 128, w_k, g_k),
            (second, 128, 128, w_v, g_v),
        ):
            block = source[top : top + 64, left : left + width]
            where = rows_at(group * width, width)
            grad[:, where] = block * column
            product = block * weight[:, where].astype(F32)
            for tile in range(width // 128):
                products = products + product[:, tile * 128 : tile * 128 + 128]
    g_out[:, 0:256] = first[320:384]
    g_out[:, 256:512] = first[384:448]
    g_out[:, 512:768] = second[320:384]
    g_out[:, 768:1024] = second[384:448]
    sums = jnp.sum(products, axis=1, keepdims=True)
    row = jnp.sum(jnp.where(lane == line, sums, 0.0), axis=0, keepdims=True)
    g_gain[0:8, :] = jnp.broadcast_to(row, (8, 128))
    g_gain[8:24, :] = extra


def ffn_core(at, keep_a, got_a, keep_b, got_b, *outs):
    x = at[2]
    step_now = pl.program_id(0)

    def write(keep, got):
        for step in range(4):
            where = rows_at(back(x, step) * 128, 128)
            outs[step][...] = (
                keep[:, where].astype(F32) + got[:, where].astype(F32)
            ).astype(BF16)

    @pl.when(step_now < 8)
    def _():
        write(keep_a, got_a)

    @pl.when(step_now >= 8)
    def _():
        write(keep_b, got_b)


def ffn_core_call(at, keep_a, got_a, keep_b, got_b):
    spec_a = pl.BlockSpec((288, 512), lambda i: (jnp.minimum(i, 7), 0))
    spec_b = pl.BlockSpec((288, 512), lambda i: (jnp.maximum(i - 8, 0), 0))
    return pl.pallas_call(
        ffn_core,
        out_shape=[shape((3456, 128), BF16)] * 4,
        grid=(12,),
        in_specs=[pl.BlockSpec(memory_space=pltpu.SMEM), spec_a, spec_a, spec_b, spec_b],
        out_specs=[pl.BlockSpec((288, 128), lambda i: (i, 0))] * 4,
        compiler_params=pltpu.CompilerParams(vmem_limit_bytes=50 * 1024 * 1024),
    )(at, keep_a, got_a, keep_b, got_b)


def ffn_x(at, *refs):
    parts, outs = refs[0:4], refs[4:8]
    for section in range(3):
        for piece in range(4):
            first = section * 1152 + piece * 288
            total = parts[0][first : first + 288, :].astype(F32)
            for part in parts[1:]:
                total = total + part[first : first + 288, :].astype(F32)
            outs[piece][section * 288 : section * 288 + 288, :] = total.astype(BF16)


def ffn_z(at, *refs):
    refs[4][...] = sum_parts(refs[0:4]).astype(BF16)


def ffn_join(at, *refs):
    parts, out = refs[0:4], refs[4]
    x = at[2]
    for step in range(4):
        out[:, rows_at(back(x, step) * 128, 128)] = parts[step][...]


def ffn_out(at, own, other, *outs):
    core = at[3]
    for section in range(3):
        rows = slice(section * 288, section * 288 + 288)
        outs[section][:, rows_at(core * 512, 512)] = own[rows, :].astype(F32)
        outs[section][:, rows_at((1 - core) * 512, 512)] = other[rows, :].astype(F32)


def on_device(
    tokens,
    lengths,
    cotangent,
    attention_gain,
    query_weight,
    key_weight,
    value_weight,
    query_gain,
    key_gain,
    out_weight,
    middle_gain,
    gate_weight,
    up_weight,
    down_weight,
):
    place = lax.axis_index("fsdp")
    copy = lax.axis_index("replica")
    y, z, x, core = place // 4, place % 4, copy // 2, copy % 2
    at = jnp.stack([y, z, x, core]).astype(jnp.int32)

    def line_of(gain):
        return jnp.pad(gain.astype(F32), (0, 128 - gain.shape[0]))[None, :]

    gains = jnp.concatenate(
        [line_of(attention_gain), line_of(middle_gain), line_of(query_gain), line_of(key_gain)]
        + [jnp.zeros((4, 128), F32)],
        axis=0,
    )

    normed, *sends = run(
        prepare,
        [((128, 1024), BF16)] + [((80, 512), BF16)] * 4,
        (at, gains, tokens, query_weight, key_weight, value_weight),
    )
    w_rows = jnp.concatenate(
        [sends[0]] + [to_y(sends[step], step) for step in (1, 2, 3)], axis=0
    )
    x_parts = gather(to_y, normed)
    w_parts = gather(to_z, w_rows)
    out_parts = gather(to_z, out_weight)
    ct_parts = gather(to_y, cotangent)

    ffn_own = jnp.concatenate([gate_weight.T, up_weight.T, down_weight], axis=0)
    ffn_parts = gather(to_z, ffn_own)
    w_gate, w_up, w_down = (
        jnp.concatenate([part[i * 288 : i * 288 + 288] for part in ffn_parts], axis=0)
        for i in range(3)
    )

    lane = np.arange(128)
    inverse_period = ROPE_BASE ** (-2.0 * (lane % 32) / HEAD_DIM)
    sign = np.where(lane % 64 < 32, -1.0, 1.0)
    blocks = jnp.arange(512, dtype=jnp.int32)
    places = (blocks // 128 * 4 + z) * 128 + blocks % 128
    passed_rows = jnp.zeros_like(places)
    end = jnp.zeros((), jnp.int32)
    for i in range(4):
        end = end + lengths[0, i]
        passed_rows = passed_rows + jnp.where(places >= end, lengths[0, i], 0)
    starts = jnp.pad(passed_rows.reshape(4, 128), ((0, 4), (0, 0)))
    angles = (places - passed_rows).astype(F32)[:, None] * jnp.asarray(inverse_period, F32)
    cosine = jnp.cos(angles)
    sine = jnp.sin(angles) * jnp.asarray(sign, F32)

    query, key_value, raw, x_full, w_full, gain_tile = run(
        project,
        [
            ((512, 256), BF16),
            ((512, 256), BF16),
            ((512, 384), F32),
            ((512, 1024), BF16),
            ((1024, 512), BF16),
            ((16, 128), F32),
        ],
        (at, *x_parts, *w_parts, cosine, sine),
    )
    kv_parts = gather(to_z, key_value)
    keys, values, attended, inverse, w_out, *mixed = run(
        attend,
        [
            ((2048, 128), BF16),
            ((2048, 128), BF16),
            ((512, 256), BF16),
            ((8, 256), F32),
            ((256, 1024), BF16),
        ]
        + [((128, 1024), BF16)] * 4,
        (at, query, *kv_parts, *out_parts, starts),
        [pltpu.VMEM((128, 2048), BF16), pltpu.VMEM((512, 1024), F32)],
    )
    middle, normed_mid = run(
        join_middle,
        [((128, 1024), F32), ((128, 1024), BF16)],
        (at, tokens, gain_tile, *scatter(to_y, mixed)),
    )

    mid_full = jnp.concatenate(gather(to_y, normed_mid), axis=0)
    ct_full = jnp.concatenate(ct_parts, axis=0)
    gate = nt(mid_full, w_gate)
    up = nt(mid_full, w_up)
    d_hidden = nt(ct_full, w_down)
    sigmoid = 1.0 / (1.0 + jnp.exp(-gate))
    silu = gate * sigmoid
    hidden = (silu * up).astype(BF16)
    d_gate = (d_hidden * up * sigmoid * (1.0 + gate * (1.0 - sigmoid))).astype(BF16)
    d_up = (d_hidden * silu).astype(BF16)
    d_normed = (nn(d_gate, w_gate) + nn(d_up, w_up)).astype(BF16)
    d_normed_parts = scatter(to_y, [d_normed[i * 128 : i * 128 + 128] for i in range(4)])
    d_middle, d_low, middle_line = run(
        back_middle,
        [((128, 1024), F32), ((128, 1024), BF16), ((8, 1024), F32)],
        (at, middle, cotangent, gain_tile, *d_normed_parts),
    )
    d_low_parts = gather(to_y, d_low)

    result = nn(hidden, w_down).astype(BF16)
    result_parts = scatter(to_y, [result[i * 128 : i * 128 + 128] for i in range(4)])
    block_output = (middle + sum_parts(result_parts)).astype(BF16)

    def halves(value):
        return [
            lax.dynamic_slice_in_dim(value, which * 512, 512, 1) for which in (1 - core, core)
        ]

    def tn(left, right):
        product = lax.dot_general(
            left, right, (((0,), (0,)), ((), ())), preferred_element_type=F32
        )
        return product.astype(BF16)

    d_both = jnp.concatenate([d_gate, d_up], axis=1)
    mid_send, mid_keep = halves(mid_full)
    ct_send, ct_keep = halves(ct_full)
    got_a = to_core(tn(d_both, mid_send))
    got_b = to_core(tn(hidden, ct_send))
    ffn_split = ffn_core_call(at, tn(d_both, mid_keep), got_a, tn(hidden, ct_keep), got_b)
    ffn_rows = run(ffn_x, [((864, 128), BF16)] * 4, (at, *scatter(to_x, ffn_split)))
    (ffn_sum,) = run(ffn_z, [((864, 128), BF16)], (at, *scatter(to_z, ffn_rows)))
    (ffn_half,) = run(ffn_join, [((864, 512), BF16)], (at, *gather(to_x, ffn_sum)))
    g_gate, g_up, g_down = run(
        ffn_out, [((288, 1024), F32)] * 3, (at, ffn_half, to_core(ffn_half))
    )

    *d_kv, d_query, query_line, out_grad = run(
        attend_back,
        [((512, 256), BF16)] * 4
        + [((512, 256), BF16), ((8, 128), F32), ((256, 1024), F32)],
        (at, query, keys, values, attended, inverse, w_out, starts)
        + (*d_low_parts, raw, cosine, sine, gain_tile),
        [
            pltpu.VMEM((512, 1024), BF16),
            pltpu.VMEM((2048, 128), F32),
            pltpu.VMEM((2048, 128), F32),
            pltpu.VMEM((128, 2048), BF16),
            pltpu.VMEM((512, 256), F32),
        ],
    )
    d_kv_parts = scatter(to_z, d_kv)
    d_joint, keep, send = run(
        weight_back,
        [((512, 512), BF16), ((4, 448, 256), BF16), ((4, 448, 256), BF16)],
        (at, raw, cosine, sine, gain_tile, d_query, query_line, middle_line)
        + (*d_kv_parts, x_full, out_grad),
        [pltpu.VMEM((1024, 512), F32), pltpu.VMEM((256, 128), F32)],
    )
    tail_parts = run(tail_core, [((448, 256), BF16)] * 4, (at, keep, to_core(send)))
    d_in_blocks = run(
        input_back,
        [((128, 1024), BF16)] * 4,
        (at, d_joint, w_full),
        [pltpu.VMEM((512, 1024), F32)],
    )
    *tail_blocks, tail_rows = run(
        tail_z,
        [((80, 256), BF16)] * 4 + [((128, 256), BF16)],
        (at, *scatter(to_z, tail_parts)),
        [pltpu.VMEM((448, 256), F32)],
    )
    tail_joint = jnp.concatenate(scatter(to_y, tail_blocks) + [tail_rows], axis=0)
    (tail_half,) = run(tail_x, [((448, 256), BF16)], (at, *gather(to_x, tail_joint)))
    g_query, g_key, g_value, g_out, g_gain = run(
        tail_out,
        [
            ((64, 1024), F32),
            ((64, 512), F32),
            ((64, 512), F32),
            ((64, 1024), F32),
            ((24, 128), F32),
        ],
        (at, tail_half, to_core(tail_half), gains, query_weight, key_weight, value_weight),
    )
    (tokens_grad,) = run(
        join_tokens,
        [((128, 1024), F32)],
        (at, tokens, d_middle, *scatter(to_y, d_in_blocks)),
    )
    return (
        block_output,
        tokens_grad,
        g_gain[0, 0:64],
        g_query,
        g_key,
        g_value,
        g_gain[9, 0:4],
        g_gain[10, 0:4],
        g_out,
        g_gain[8, 0:64],
        g_gate.T,
        g_up.T,
        g_down,
    )


def solution(mesh):
    return jax.shard_map(
        on_device,
        mesh=mesh,
        in_specs=(
            P(("replica", "fsdp"), None),
            P("replica", None),
            P(("replica", "fsdp"), None),
            P("fsdp"),
            P("fsdp", None),
            P("fsdp", None),
            P("fsdp", None),
            P("fsdp"),
            P("fsdp"),
            P("fsdp", None),
            P("fsdp"),
            P(None, "fsdp"),
            P(None, "fsdp"),
            P("fsdp", None),
        ),
        out_specs=(
            P(("replica", "fsdp"), None),
            P(("replica", "fsdp"), None),
            P("fsdp"),
            P("fsdp", None),
            P("fsdp", None),
            P("fsdp", None),
            P("fsdp"),
            P("fsdp"),
            P("fsdp", None),
            P("fsdp"),
            P(None, "fsdp"),
            P(None, "fsdp"),
            P("fsdp", None),
        ),
        check_vma=False,
    )
```

time: 1440 us -> 401 us (0.28)
  waiting for transfers between devices: 1110 us -> 206 us
  blocking collectives: 85.4 us -> 0 us
  starting transfers between devices: 0.76 us -> 79.6 us
  matrix products: 87.7 us -> 25 us
  Pallas kernels: 0 us -> 47 us
  local copies, waits for them, and re-layouts: 59.6 us -> 20.6 us
  loops' own time: 38.1 us -> 0 us
  other arithmetic: 37.4 us -> 10.5 us
    reduce_scatter x7 -> x0, waiting for transfers between devices: 549 us -> none  [the longest x1 91 us: on_device(): lax.psum_scatter(term_gate.astype(jnp.bfloat16), 'fsdp', scatter_dimensio...]
    all_gather x9 -> x0, waiting for transfers between devices: 385 us -> none  [the longest x1 75.9 us: on_device(): lax.all_gather(gate_weight, 'fsdp', axis=1, tiled=True)]
    ppermute x0 -> x65, waiting for transfers between devices: none -> 206 us  [the longest x21 117 us: to_z(): return lax.ppermute(value, 'fsdp', yz_perm(0, step))]
    unnamed x20 -> x0, waiting for transfers between devices: 87.8 us -> none
    ppermute x0 -> x65, starting transfers between devices: none -> 79.6 us  [the longest x30 38.9 us: to_y(): return lax.ppermute(value, 'fsdp', yz_perm(step, 0))]
    convert_element_type x1 -> x0, waiting for transfers between devices: 74.4 us -> none  [on_device(): value_grad.reshape(row_count, KV_HEADS * HEAD_DIM).astype(jnp.bfloat16)]
    unnamed x2 -> x0, blocking collectives: 66.7 us -> none
    dot_general x28 -> x10, matrix products: 87.7 us -> 25 us  [the longest x4 11 us: tn(): lax.dot_general(left, right, (((0,), (0,)), ((), ())), preferred_element_...]
  transfers between devices with their start and end apart: 19 -> 65, of which waited for: 19 -> 34; matrix products, arithmetic and copies ran while one was open for 8% -> 8% of each run, Pallas kernels for 0% -> 11%
where the time goes in v1:
time: 401 us; the launch traced here: 394 us
  waiting for transfers between devices  206 us (51%)
  starting transfers between devices  79.6 us (20%)
  Pallas kernels  47 us (12%)
  matrix products  25 us (6%)
  local copies, waits for them, and re-layouts  20.6 us (5%)
  other arithmetic  10.5 us (3%)
  between operations  4.35 us (1%)
    ppermute x21, waiting for transfers between devices, to_z(): return lax.ppermute(value, 'fsdp', yz_perm(0, step))  117 us
    ppermute x30, waiting for transfers between devices, to_y(): return lax.ppermute(value, 'fsdp', yz_perm(step, 0))  65 us
    pallas_call x17, Pallas kernels, run(): pl.pallas_call(kernel, out_shape=[shape(dims, dtype) for dims, dtype in o...  39.3 us
    ppermute x30, starting transfers between devices, to_y(): return lax.ppermute(value, 'fsdp', yz_perm(step, 0))  38.9 us
    ppermute x9, waiting for transfers between devices, to_x(): return lax.ppermute(value, 'replica', pairs)  24 us
    ppermute x21, starting transfers between devices, to_z(): return lax.ppermute(value, 'fsdp', yz_perm(0, step))  20.3 us
    ppermute x9, starting transfers between devices, to_x(): return lax.ppermute(value, 'replica', pairs)  12.8 us
    unnamed x97, local copies, waits for them, and re-layouts  11 us
  transfers between devices with their start and end apart: 65, of which 34 were waited for; matrix products, arithmetic and copies ran while one was open for 8% of the time, Pallas kernels for 11%

profile of v1, /device:TPU:7, one launch (start us, length us, event | category | flops | bytes accessed | tf_op | source)
XLA Modules:
  0.0 393.7 jit_solution(16174177486239166867)
XLA Ops:
  16.7 3.5 collective-permute-done.3
  20.2 3.6 collective-permute-start.5
  26.9 3.3 collective-permute-start.7
  36.5 4.9 %collective-permute-done.7.refs_6_ = bf16[320,512]{1,0:T(8,128)(2,1)S(1)} collective-permute-done((bf16[320,512]{1,0:T(8,128)(2,1)S(1)}, bf16[320,512]{1,0:T(8,128)(2,1)S(1)}, u32[]{:S(2)}, u32[]{:S(2)}) %collective-permute-start.7) | collective-permute-done | bytes 327712 | tf_op jit(solution)/shard_map/ppermute | solution.py:46
  43.9 3.9 shard_map.256
  47.8 3.4 collective-permute-start.9
  56.5 48.9 %collective-permute-done.14.refs_7_ = bf16[64,1024]{1,0:T(8,128)(2,1)S(1)} collective-permute-done((bf16[64,1024]{1,0:T(8,128)(2,1)S(1)}, bf16[64,1024]{1,0:T(8,128)(2,1)S(1)}, u32[]{:S(2)}, u32[]{:S(2)}) %collective-permute-start.14) | collective-permute-done | bytes 131104 | tf_op jit(solution)/shard_map/ppermute | solution.py:46
  110.7 5.7 %shard_map.257 = (bf16[2048,128]{1,0:T(8,128)(2,1)S(1)}, bf16[2048,128]{1,0:T(8,128)(2,1)}, bf16[512,256]{1,0:T(8,128)(2,1)S(1)}, f32[8,256]{1,0:T(8,128)S(1)}, ...) custom-call(s32[4]{0:T(128)S(1)} %pad_add_fusion.at, ...), custom_call_target="tpu_custom_call" | custom-call | tf_op jit(solution)/shard_map/pallas_call | solution.py:24
  119.4 3.3 collective-permute-done.15.refs_1_
  126.1 6.0 %collective-permute-done.17.refs_3_ = bf16[128,1024]{1,0:T(8,128)(2,1)S(1)} collective-permute-done((bf16[128,1024]{1,0:T(8,128)(2,1)S(1)}, bf16[128,1024]{1,0:T(8,128)(2,1)S(1)}, u32[]{:S(2)}, u32[]{:S(2)}) %collective-permute-start.17) | collective-permute-done | bytes 262176 | tf_op jit(solution)/shard_map/ppermute | solution.py:42
  152.8 33.0 %collective-permute-done.21 = bf16[864,1024]{1,0:T(8,128)(2,1)} collective-permute-done((bf16[864,1024]{1,0:T(8,128)(2,1)}, bf16[864,1024]{1,0:T(8,128)(2,1)}, u32[]{:S(2)}, u32[]{:S(2)}) %collective-permute-start.21) | collective-permute-done | bytes 1769504 | tf_op jit(solution)/shard_map/ppermute | solution.py:46
  190.6 6.0 %multiply_convert_fusion.1 = (bf16[512,1152]{1,0:T(8,128)(2,1)S(1)}, bf16[512,1152]{1,0:T(8,128)(2,1)S(1)}, bf16[512,1152]{1,0:T(8,128)(2,1)S(1)}) fusion(f32[512,1152]{1,0:T(8,128)S(1)} %fusion.5, f32[512,1152]{1,0:T(8,128)S(1)} %fusion.7, bf16[512,1024]{1,0:T(8,128)(2,1)S(1)} %constant_dynamic-update-slice_fusion.4, ...), kind=kOutput, calls=%fused_computation.9 | convolution fusion | flops 1226244096 | bytes 11665408 | tf_op jit(solution)/shard_map/dot_general | solution.py:79
  206.8 10.2 %collective-permute-done.30.refs_1_ = bf16[128,1024]{1,0:T(8,128)(2,1)S(1)} collective-permute-done((bf16[128,1024]{1,0:T(8,128)(2,1)S(1)}, bf16[128,1024]{1,0:T(8,128)(2,1)S(1)}, u32[]{:S(2)}, u32[]{:S(2)}) %collective-permute-start.30) | collective-permute-done | bytes 262176 | tf_op jit(solution)/shard_map/ppermute | solution.py:42
  217.0 4.2 %collective-permute-done.32.refs_3_ = bf16[128,1024]{1,0:T(8,128)(2,1)S(1)} collective-permute-done((bf16[128,1024]{1,0:T(8,128)(2,1)S(1)}, bf16[128,1024]{1,0:T(8,128)(2,1)S(1)}, u32[]{:S(2)}, u32[]{:S(2)}) %collective-permute-start.32) | collective-permute-done | bytes 262176 | tf_op jit(solution)/shard_map/ppermute | solution.py:42
  226.1 11.0 %collective-permute-done.33.refs_1_ = bf16[128,1024]{1,0:T(8,128)(2,1)S(1)} collective-permute-done((bf16[128,1024]{1,0:T(8,128)(2,1)S(1)}, bf16[128,1024]{1,0:T(8,128)(2,1)S(1)}, u32[]{:S(2)}, u32[]{:S(2)}) %collective-permute-start.33) | collective-permute-done | bytes 262176 | tf_op jit(solution)/shard_map/ppermute | solution.py:42
  237.5 10.8 %shard_map.260 = (bf16[512,256]{1,0:T(8,128)(2,1)S(1)}, bf16[512,256]{1,0:T(8,128)(2,1)S(1)}, bf16[512,256]{1,0:T(8,128)(2,1)S(1)}, bf16[512,256]{1,0:T(8,128)(2...) custom-call(s32[4]{0:T(128)S(1)} %pad_add_fusion.at, ...), custom_call_target="tpu_custom_call" | custom-call | tf_op jit(solution)/shard_map/pallas_call | solution.py:24
  256.2 7.8 %collective-permute-done.38.refs_3_ = bf16[512,256]{1,0:T(8,128)(2,1)S(1)} collective-permute-done((bf16[512,256]{1,0:T(8,128)(2,1)S(1)}, bf16[512,256]{1,0:T(8,128)(2,1)S(1)}, u32[]{:S(2)}, u32[]{:S(2)}) %collective-permute-start.38) | collective-permute-done | bytes 262176 | tf_op jit(solution)/shard_map/ppermute | solution.py:46
  264.0 4.0 %shard_map.261 = (bf16[512,512]{1,0:T(8,128)(2,1)S(1)}, bf16[4,448,256]{2,1,0:T(8,128)(2,1)S(1)}, bf16[4,448,256]{2,1,0:T(8,128)(2,1)}) custom-call(s32[4]{0:T(128)S(1)} %pad_add_fusion.at, f32[512,384]{1,0:T(8,128)S(1)} %copy-done, f32[512,128]{1,0:T(8,128)S(1)} %get-tuple-element.165.refs_8_.refs_5_.cosine, ...), custom_call_target="tpu_custom_call" | custom-call | tf_op jit(solution)/shard_map/pallas_call | solution.py:24
  269.5 3.4 convolution_convert_fusion.3.keep_b
  274.3 2.9 convolution_convert_fusion.1.keep_a
  277.3 7.7 %shard_map.268 = (bf16[3456,128]{1,0:T(8,128)(2,1)S(1)}, bf16[3456,128]{1,0:T(8,128)(2,1)S(1)}, bf16[3456,128]{1,0:T(8,128)(2,1)S(1)}, bf16[3456,128]{1,0:T(8,128)(2,1)S(1)}) custom-call(s32[4]{0:T(128)S(1)} %pad_add_fusion.at, bf16[2304,512]{1,0:T(8,128)(2,1)} %convolution_convert_fusion.1.keep_a, bf16[2304,512]{1,0:T(8,128)(2,1)} %collective-permute-done.53.got_a, ...), custom_call_target="tpu_custom_call" | custom-call | tf_op jit(solution)/shard_map/pallas_call | solution.py:485
  290.8 5.0 %collective-permute-done.44.refs_2_ = bf16[448,256]{1,0:T(8,128)(2,1)S(1)} collective-permute-done((bf16[448,256]{1,0:T(8,128)(2,1)S(1)}, bf16[448,256]{1,0:T(8,128)(2,1)S(1)}, u32[]{:S(2)}, u32[]{:S(2)}) %collective-permute-start.44) | collective-permute-done | bytes 229408 | tf_op jit(solution)/shard_map/ppermute | solution.py:46
  295.8 6.5 %collective-permute-done.45.refs_3_ = bf16[448,256]{1,0:T(8,128)(2,1)S(1)} collective-permute-done((bf16[448,256]{1,0:T(8,128)(2,1)S(1)}, bf16[448,256]{1,0:T(8,128)(2,1)S(1)}, u32[]{:S(2)}, u32[]{:S(2)}) %collective-permute-start.45) | collective-permute-done | bytes 229408 | tf_op jit(solution)/shard_map/ppermute | solution.py:46
  303.0 3.5 collective-permute-start.46
  307.6 3.5 collective-permute-done.47
  311.1 15.0 %collective-permute-done.55.refs_1_ = bf16[3456,128]{1,0:T(8,128)(2,1)S(1)} collective-permute-done((bf16[3456,128]{1,0:T(8,128)(2,1)S(1)}, bf16[3456,128]{1,0:T(8,128)(2,1)S(1)}, u32[]{:S(2)}, u32[]{:S(2)}) %collective-permute-start.55) | collective-permute-done | bytes 884768 | tf_op jit(solution)/shard_map/ppermute | solution.py:51
  331.9 3.4 collective-permute-start.49
  336.0 5.7 %collective-permute-done.60.refs_3_ = bf16[864,128]{1,0:T(8,128)(2,1)S(1)} collective-permute-done((bf16[864,128]{1,0:T(8,128)(2,1)S(1)}, bf16[864,128]{1,0:T(8,128)(2,1)S(1)}, u32[]{:S(2)}, u32[]{:S(2)}) %collective-permute-start.60) | collective-permute-done | bytes 221216 | tf_op jit(solution)/shard_map/ppermute | solution.py:46
  342.4 4.4 %collective-permute-start.61 = (bf16[864,128]{1,0:T(8,128)(2,1)S(1)}, bf16[864,128]{1,0:T(8,128)(2,1)S(1)}, u32[]{:S(2)}, u32[]{:S(2)}) collective-permute-start(bf16[864,128]{1,0:T(8,128)(2,1)S(1)} %shard_map.270.refs_0_), channel_id=1, source_target_pairs={{0,32},{16,48},{32,64},{48,80},{64,96},{80,112},{96,0},{112,16},{1... | collective-permute-start | bytes 663560 | tf_op jit(solution)/shard_map/ppermute | solution.py:51
  349.3 6.3 %collective-permute-done.61.refs_1_ = bf16[864,128]{1,0:T(8,128)(2,1)S(1)} collective-permute-done((bf16[864,128]{1,0:T(8,128)(2,1)S(1)}, bf16[864,128]{1,0:T(8,128)(2,1)S(1)}, u32[]{:S(2)}, u32[]{:S(2)}) %collective-permute-start.61) | collective-permute-done | bytes 221216 | tf_op jit(solution)/shard_map/ppermute | solution.py:51
  367.4 3.2 collective-permute-start.39
  378.8 7.6 %collective-permute-done.41.refs_3_ = bf16[128,1024]{1,0:T(8,128)(2,1)S(1)} collective-permute-done((bf16[128,1024]{1,0:T(8,128)(2,1)S(1)}, bf16[128,1024]{1,0:T(8,128)(2,1)S(1)}, u32[]{:S(2)}, u32[]{:S(2)}) %collective-permute-start.41) | collective-permute-done | bytes 262176 | tf_op jit(solution)/shard_map/ppermute | solution.py:42
  (246 shorter events, 137.3 us)
Async XLA Ops:
  6.4 23.8 %collective-permute-start = (bf16[128,1024]{1,0:T(8,128)(2,1)S(1)}, bf16[128,1024]{1,0:T(8,128)(2,1)S(1)}, u32[]{:S(2)}, u32[]{:S(2)}) collective-permute-start(bf16[128,1024]{1,0:T(8,128)(2,1)S(1)} %get-tuple-element.77.refs_0_), channel_id=1, source_target_pairs={{0,4},{1,5},{2,6},{3,7},{4,8},{5,9},{6,10},{7,11},{8,12},{9,13},{1... | collective-permute-start | bytes 786440 | tf_op jit(solution)/shard_map/ppermute | solution.py:42
  7.8 27.5 %collective-permute-start.1 = (bf16[128,1024]{1,0:T(8,128)(2,1)S(1)}, bf16[128,1024]{1,0:T(8,128)(2,1)S(1)}, u32[]{:S(2)}, u32[]{:S(2)}) collective-permute-start(bf16[128,1024]{1,0:T(8,128)(2,1)S(1)} %get-tuple-element.77.refs_0_), channel_id=1, source_target_pairs={{0,8},{1,9},{2,10},{3,11},{4,12},{5,13},{6,14},{7,15},{8,0},{9,1},... | collective-permute-start | bytes 786440 | tf_op jit(solution)/shard_map/ppermute | solution.py:42
  10.4 25.7 %collective-permute-start.2 = (bf16[128,1024]{1,0:T(8,128)(2,1)S(1)}, bf16[128,1024]{1,0:T(8,128)(2,1)S(1)}, u32[]{:S(2)}, u32[]{:S(2)}) collective-permute-start(bf16[128,1024]{1,0:T(8,128)(2,1)S(1)} %get-tuple-element.77.refs_0_), channel_id=1, source_target_pairs={{0,12},{1,13},{2,14},{3,15},{4,0},{5,1},{6,2},{7,3},{8,4},{9,5},{1... | collective-permute-start | bytes 786440 | tf_op jit(solution)/shard_map/ppermute | solution.py:42
  26.9 14.5 %collective-permute-start.7 = (bf16[320,512]{1,0:T(8,128)(2,1)S(1)}, bf16[320,512]{1,0:T(8,128)(2,1)S(1)}, u32[]{:S(2)}, u32[]{:S(2)}) collective-permute-start(bf16[320,512]{1,0:T(8,128)(2,1)S(1)} %constant_dynamic-update-slice_fusion.refs_4_), channel_id=1, source_target_pairs={{0,2},{1,3},{2,0},{3,1},{4,6},{5,7},{6,4},{7,5},{8,10},{9,11},{10,... | collective-permute-start | bytes 983048 | tf_op jit(solution)/shard_map/ppermute | solution.py:46
  35.3 19.2 %collective-permute-start.12 = (bf16[64,1024]{1,0:T(8,128)(2,1)}, bf16[64,1024]{1,0:T(8,128)(2,1)S(1)}, u32[]{:S(2)}, u32[]{:S(2)}) collective-permute-start(bf16[64,1024]{1,0:T(8,128)(2,1)} %refs_4_.1), channel_id=1, source_target_pairs={{0,1},{1,2},{2,3},{3,0},{4,5},{5,6},{6,7},{7,4},{8,9},{9,10},{10,1... | collective-permute-start | bytes 393224 | tf_op jit(solution)/shard_map/ppermute | solution.py:46
  36.1 20.4 %collective-permute-start.13 = (bf16[64,1024]{1,0:T(8,128)(2,1)}, bf16[64,1024]{1,0:T(8,128)(2,1)S(1)}, u32[]{:S(2)}, u32[]{:S(2)}) collective-permute-start(bf16[64,1024]{1,0:T(8,128)(2,1)} %refs_4_.1), channel_id=1, source_target_pairs={{0,2},{1,3},{2,0},{3,1},{4,6},{5,7},{6,4},{7,5},{8,10},{9,11},{10,... | collective-permute-start | bytes 393224 | tf_op jit(solution)/shard_map/ppermute | solution.py:46
  47.8 57.9 %collective-permute-start.9 = (bf16[512,256]{1,0:T(8,128)(2,1)S(1)}, bf16[512,256]{1,0:T(8,128)(2,1)S(1)}, u32[]{:S(2)}, u32[]{:S(2)}) collective-permute-start(bf16[512,256]{1,0:T(8,128)(2,1)S(1)} %get-tuple-element.84.refs_0_), channel_id=1, source_target_pairs={{0,1},{1,2},{2,3},{3,0},{4,5},{5,6},{6,7},{7,4},{8,9},{9,10},{10,1... | collective-permute-start | bytes 786440 | tf_op jit(solution)/shard_map/ppermute | solution.py:46
  52.6 96.4 %collective-permute-start.23 = (bf16[864,1024]{1,0:T(8,128)(2,1)}, bf16[864,1024]{1,0:T(8,128)(2,1)}, u32[]{:S(2)}, u32[]{:S(2)}) collective-permute-start(bf16[864,1024]{1,0:T(8,128)(2,1)} %pad_maximum_fusion.4), channel_id=1, source_target_pairs={{0,3},{1,0},{2,1},{3,2},{4,7},{5,4},{6,5},{7,6},{8,11},{9,8},{10,9... | collective-permute-start | bytes 5308424 | tf_op jit(solution)/shard_map/ppermute | solution.py:46
  52.8 57.9 %collective-permute-start.10 = (bf16[512,256]{1,0:T(8,128)(2,1)S(1)}, bf16[512,256]{1,0:T(8,128)(2,1)S(1)}, u32[]{:S(2)}, u32[]{:S(2)}) collective-permute-start(bf16[512,256]{1,0:T(8,128)(2,1)S(1)} %get-tuple-element.84.refs_0_), channel_id=1, source_target_pairs={{0,2},{1,3},{2,0},{3,1},{4,6},{5,7},{6,4},{7,5},{8,10},{9,11},{10,... | collective-permute-start | bytes 786440 | tf_op jit(solution)/shard_map/ppermute | solution.py:46
  54.4 56.2 %collective-permute-start.11 = (bf16[512,256]{1,0:T(8,128)(2,1)S(1)}, bf16[512,256]{1,0:T(8,128)(2,1)S(1)}, u32[]{:S(2)}, u32[]{:S(2)}) collective-permute-start(bf16[512,256]{1,0:T(8,128)(2,1)S(1)} %get-tuple-element.84.refs_0_), channel_id=1, source_target_pairs={{0,3},{1,0},{2,1},{3,2},{4,7},{5,4},{6,5},{7,6},{8,11},{9,8},{10,9... | collective-permute-start | bytes 786440 | tf_op jit(solution)/shard_map/ppermute | solution.py:46
  56.5 49.0 %collective-permute-start.14 = (bf16[64,1024]{1,0:T(8,128)(2,1)S(1)}, bf16[64,1024]{1,0:T(8,128)(2,1)S(1)}, u32[]{:S(2)}, u32[]{:S(2)}) collective-permute-start(bf16[64,1024]{1,0:T(8,128)(2,1)S(1)} %copy-done.17), channel_id=1, source_target_pairs={{0,3},{1,0},{2,1},{3,2},{4,7},{5,4},{6,5},{7,6},{8,11},{9,8},{10,9... | collective-permute-start | bytes 393224 | tf_op jit(solution)/shard_map/ppermute | solution.py:46
  105.5 45.5 %collective-permute-start.22 = (bf16[864,1024]{1,0:T(8,128)(2,1)}, bf16[864,1024]{1,0:T(8,128)(2,1)}, u32[]{:S(2)}, u32[]{:S(2)}) collective-permute-start(bf16[864,1024]{1,0:T(8,128)(2,1)} %pad_maximum_fusion.4), channel_id=1, source_target_pairs={{0,2},{1,3},{2,0},{3,1},{4,6},{5,7},{6,4},{7,5},{8,10},{9,11},{10,... | collective-permute-start | bytes 5308424 | tf_op jit(solution)/shard_map/ppermute | solution.py:46
  122.7 63.0 %collective-permute-start.21 = (bf16[864,1024]{1,0:T(8,128)(2,1)}, bf16[864,1024]{1,0:T(8,128)(2,1)}, u32[]{:S(2)}, u32[]{:S(2)}) collective-permute-start(bf16[864,1024]{1,0:T(8,128)(2,1)} %pad_maximum_fusion.4), channel_id=1, source_target_pairs={{0,1},{1,2},{2,3},{3,0},{4,5},{5,6},{6,7},{7,4},{8,9},{9,10},{10,1... | collective-permute-start | bytes 5308424 | tf_op jit(solution)/shard_map/ppermute | solution.py:46
  201.1 76.2 %collective-permute-start.53 = (bf16[2304,512]{1,0:T(8,128)(2,1)}, bf16[2304,512]{1,0:T(8,128)(2,1)}, u32[]{:S(2)}, u32[]{:S(2)}) collective-permute-start(bf16[2304,512]{1,0:T(8,128)(2,1)} %convolution_convert_fusion), channel_id=1, source_target_pairs={{0,16},{16,0},{32,48},{48,32},{64,80},{80,64},{96,112},{112,96},{1... | collective-permute-start | bytes 7077896 | tf_op jit(solution)/shard_map/ppermute | solution.py:55
  206.8 14.4 %collective-permute-start.32 = (bf16[128,1024]{1,0:T(8,128)(2,1)S(1)}, bf16[128,1024]{1,0:T(8,128)(2,1)S(1)}, u32[]{:S(2)}, u32[]{:S(2)}) collective-permute-start(bf16[128,1024]{1,0:T(8,128)(2,1)S(1)} %get-tuple-element.153), channel_id=1, source_target_pairs={{0,4},{1,5},{2,6},{3,7},{4,8},{5,9},{6,10},{7,11},{8,12},{9,13},{1... | collective-permute-start | bytes 786440 | tf_op jit(solution)/shard_map/ppermute | solution.py:42
  222.9 14.2 %collective-permute-start.33 = (bf16[128,1024]{1,0:T(8,128)(2,1)S(1)}, bf16[128,1024]{1,0:T(8,128)(2,1)S(1)}, u32[]{:S(2)}, u32[]{:S(2)}) collective-permute-start(bf16[128,1024]{1,0:T(8,128)(2,1)S(1)} %get-tuple-element.98.refs_0_), channel_id=1, source_target_pairs={{0,4},{1,5},{2,6},{3,7},{4,8},{5,9},{6,10},{7,11},{8,12},{9,13},{1... | collective-permute-start | bytes 786440 | tf_op jit(solution)/shard_map/ppermute | solution.py:42
  222.9 14.2 %collective-permute-start.34 = (bf16[128,1024]{1,0:T(8,128)(2,1)S(1)}, bf16[128,1024]{1,0:T(8,128)(2,1)S(1)}, u32[]{:S(2)}, u32[]{:S(2)}) collective-permute-start(bf16[128,1024]{1,0:T(8,128)(2,1)S(1)} %get-tuple-element.98.refs_0_), channel_id=1, source_target_pairs={{0,8},{1,9},{2,10},{3,11},{4,12},{5,13},{6,14},{7,15},{8,0},{9,1},... | collective-permute-start | bytes 786440 | tf_op jit(solution)/shard_map/ppermute | solution.py:42
  248.9 15.1 %collective-permute-start.38 = (bf16[512,256]{1,0:T(8,128)(2,1)S(1)}, bf16[512,256]{1,0:T(8,128)(2,1)S(1)}, u32[]{:S(2)}, u32[]{:S(2)}) collective-permute-start(bf16[512,256]{1,0:T(8,128)(2,1)S(1)} %get-tuple-element.105), channel_id=1, source_target_pairs={{0,1},{1,2},{2,3},{3,0},{4,5},{5,6},{6,7},{7,4},{8,9},{9,10},{10,1... | collective-permute-start | bytes 786440 | tf_op jit(solution)/shard_map/ppermute | solution.py:46
  251.6 25.6 %collective-permute-start.54 = (bf16[1152,512]{1,0:T(8,128)(2,1)}, bf16[1152,512]{1,0:T(8,128)(2,1)}, u32[]{:S(2)}, u32[]{:S(2)}) collective-permute-start(bf16[1152,512]{1,0:T(8,128)(2,1)} %convolution_convert_fusion.2), channel_id=1, source_target_pairs={{0,16},{16,0},{32,48},{48,32},{64,80},{80,64},{96,112},{112,96},{1... | collective-permute-start | bytes 3538952 | tf_op jit(solution)/shard_map/ppermute | solution.py:55
  273.7 14.6 %collective-permute-start.43 = (bf16[448,256]{1,0:T(8,128)(2,1)S(1)}, bf16[448,256]{1,0:T(8,128)(2,1)S(1)}, u32[]{:S(2)}, u32[]{:S(2)}) collective-permute-start(bf16[448,256]{1,0:T(8,128)(2,1)S(1)} %get-tuple-element.117), channel_id=1, source_target_pairs={{0,3},{1,0},{2,1},{3,2},{4,7},{5,4},{6,5},{7,6},{8,11},{9,8},{10,9... | collective-permute-start | bytes 688136 | tf_op jit(solution)/shard_map/ppermute | solution.py:46
  285.0 41.2 %collective-permute-start.55 = (bf16[3456,128]{1,0:T(8,128)(2,1)S(1)}, bf16[3456,128]{1,0:T(8,128)(2,1)S(1)}, u32[]{:S(2)}, u32[]{:S(2)}) collective-permute-start(bf16[3456,128]{1,0:T(8,128)(2,1)S(1)} %get-tuple-element.131), channel_id=1, source_target_pairs={{0,96},{16,112},{32,0},{48,16},{64,32},{80,48},{96,64},{112,80},{1... | collective-permute-start | bytes 2654216 | tf_op jit(solution)/shard_map/ppermute | solution.py:51
  285.6 40.5 %collective-permute-start.56 = (bf16[3456,128]{1,0:T(8,128)(2,1)S(1)}, bf16[3456,128]{1,0:T(8,128)(2,1)S(1)}, u32[]{:S(2)}, u32[]{:S(2)}) collective-permute-start(bf16[3456,128]{1,0:T(8,128)(2,1)S(1)} %get-tuple-element.132), channel_id=1, source_target_pairs={{0,64},{16,80},{32,96},{48,112},{64,0},{80,16},{96,32},{112,48},{1... | collective-permute-start | bytes 2654216 | tf_op jit(solution)/shard_map/ppermute | solution.py:51
  286.5 40.0 %collective-permute-start.57 = (bf16[3456,128]{1,0:T(8,128)(2,1)S(1)}, bf16[3456,128]{1,0:T(8,128)(2,1)S(1)}, u32[]{:S(2)}, u32[]{:S(2)}) collective-permute-start(bf16[3456,128]{1,0:T(8,128)(2,1)S(1)} %get-tuple-element.133), channel_id=1, source_target_pairs={{0,32},{16,48},{32,64},{48,80},{64,96},{80,112},{96,0},{112,16},{1... | collective-permute-start | bytes 2654216 | tf_op jit(solution)/shard_map/ppermute | solution.py:51
  307.6 24.3 %collective-permute-start.48 = (bf16[80,256]{1,0:T(8,128)(2,1)S(1)}, bf16[80,256]{1,0:T(8,128)(2,1)S(1)}, u32[]{:S(2)}, u32[]{:S(2)}) collective-permute-start(bf16[80,256]{1,0:T(8,128)(2,1)S(1)} %get-tuple-element.123), channel_id=1, source_target_pairs={{0,4},{1,5},{2,6},{3,7},{4,8},{5,9},{6,10},{7,11},{8,12},{9,13},{1... | collective-permute-start | bytes 122888 | tf_op jit(solution)/shard_map/ppermute | solution.py:42
  331.9 15.7 %collective-permute-start.49 = (bf16[448,256]{1,0:T(8,128)(2,1)S(1)}, bf16[448,256]{1,0:T(8,128)(2,1)S(1)}, u32[]{:S(2)}, u32[]{:S(2)}) collective-permute-start(bf16[448,256]{1,0:T(8,128)(2,1)S(1)} %constant_dynamic-update-slice_fusion.12.own), channel_id=1, source_target_pairs={{0,32},{16,48},{32,64},{48,80},{64,96},{80,112},{96,0},{112,16},{1... | collective-permute-start | bytes 688136 | tf_op jit(solution)/shard_map/ppermute | solution.py:51
  335.3 26.4 %collective-permute-start.50 = (bf16[448,256]{1,0:T(8,128)(2,1)S(1)}, bf16[448,256]{1,0:T(8,128)(2,1)S(1)}, u32[]{:S(2)}, u32[]{:S(2)}) collective-permute-start(bf16[448,256]{1,0:T(8,128)(2,1)S(1)} %constant_dynamic-update-slice_fusion.12.own), channel_id=1, source_target_pairs={{0,64},{16,80},{32,96},{48,112},{64,0},{80,16},{96,32},{112,48},{1... | collective-permute-start | bytes 688136 | tf_op jit(solution)/shard_map/ppermute | solution.py:51
  347.6 23.8 %collective-permute-start.26 = (bf16[128,1024]{1,0:T(8,128)(2,1)S(1)}, bf16[128,1024]{1,0:T(8,128)(2,1)S(1)}, u32[]{:S(2)}, u32[]{:S(2)}) collective-permute-start(bf16[128,1024]{1,0:T(8,128)(2,1)S(1)} %get-tuple-element.158), channel_id=1, source_target_pairs={{0,4},{1,5},{2,6},{3,7},{4,8},{5,9},{6,10},{7,11},{8,12},{9,13},{1... | collective-permute-start | bytes 786440 | tf_op jit(solution)/shard_map/ppermute | solution.py:42
  355.7 15.9 %collective-permute-start.25 = (bf16[128,1024]{1,0:T(8,128)(2,1)S(1)}, bf16[128,1024]{1,0:T(8,128)(2,1)S(1)}, u32[]{:S(2)}, u32[]{:S(2)}) collective-permute-start(bf16[128,1024]{1,0:T(8,128)(2,1)S(1)} %get-tuple-element.159), channel_id=1, source_target_pairs={{0,8},{1,9},{2,10},{3,11},{4,12},{5,13},{6,14},{7,15},{8,0},{9,1},... | collective-permute-start | bytes 786440 | tf_op jit(solution)/shard_map/ppermute | solution.py:42
  357.0 15.0 %collective-permute-start.24 = (bf16[128,1024]{1,0:T(8,128)(2,1)S(1)}, bf16[128,1024]{1,0:T(8,128)(2,1)S(1)}, u32[]{:S(2)}, u32[]{:S(2)}) collective-permute-start(bf16[128,1024]{1,0:T(8,128)(2,1)S(1)} %get-tuple-element.157), channel_id=1, source_target_pairs={{0,12},{1,13},{2,14},{3,15},{4,0},{5,1},{6,2},{7,3},{8,4},{9,5},{1... | collective-permute-start | bytes 786440 | tf_op jit(solution)/shard_map/ppermute | solution.py:42
  361.7 29.1 %collective-permute-start.64 = (bf16[864,512]{1,0:T(8,128)(2,1)S(1)}, bf16[864,512]{1,0:T(8,128)(2,1)S(1)}, u32[]{:S(2)}, u32[]{:S(2)}) collective-permute-start(bf16[864,512]{1,0:T(8,128)(2,1)S(1)} %shard_map.271.own), channel_id=1, source_target_pairs={{0,16},{16,0},{32,48},{48,32},{64,80},{80,64},{96,112},{112,96},{1... | collective-permute-start | bytes 2654216 | tf_op jit(solution)/shard_map/ppermute | solution.py:55
  371.6 14.9 %collective-permute-start.41 = (bf16[128,1024]{1,0:T(8,128)(2,1)S(1)}, bf16[128,1024]{1,0:T(8,128)(2,1)S(1)}, u32[]{:S(2)}, u32[]{:S(2)}) collective-permute-start(bf16[128,1024]{1,0:T(8,128)(2,1)S(1)} %get-tuple-element.113), channel_id=1, source_target_pairs={{0,4},{1,5},{2,6},{3,7},{4,8},{5,9},{6,10},{7,11},{8,12},{9,13},{1... | collective-permute-start | bytes 786440 | tf_op jit(solution)/shard_map/ppermute | solution.py:42
  372.0 16.1 %collective-permute-start.52 = (bf16[448,256]{1,0:T(8,128)(2,1)S(1)}, bf16[448,256]{1,0:T(8,128)(2,1)S(1)}, u32[]{:S(2)}, u32[]{:S(2)}) collective-permute-start(bf16[448,256]{1,0:T(8,128)(2,1)S(1)} %shard_map.266.own), channel_id=1, source_target_pairs={{0,16},{16,0},{32,48},{48,32},{64,80},{80,64},{96,112},{112,96},{1... | collective-permute-start | bytes 688136 | tf_op jit(solution)/shard_map/ppermute | solution.py:55
  (75 other events, 1115.3 us)
